TPU v7x, 512 devices: a whole 4x4x16 slice. The times are simulated.
512 devices in a mesh: tm: 32 (over x_lo, z), tile: 8 (over y, core), plane: 2 (over x_hi).
Axes of the slice: x: 4 (x_hi: 2, x_lo: 2; x = x_hi * 2 + x_lo), y: 4, z: 16, core: 2. Of those that a mesh axis runs over, the one named last changes fastest.
Arguments:
- movie: bfloat16 [8, 8192, 8192], P(None, ('tile', 'plane'), 'tm'), may hold values from 0 to 1
- footprints: float32 [16, 8, 8192], P(None, None, ('tile', 'plane')), may hold values from 0 to 0.4
- traces: float32 [128, 8192], P(None, 'tm'), may hold values from 0 to 0.4
- patch_counts: int32 [8], replicated, may hold values from 1 to 16, 64 in all
- slot_neuron: int32 [128], replicated, may hold values from 0 to 127, each once
Outputs:
- new_footprints: float32 [16, 8, 8192], P(None, None, ('tile', 'plane'))
- new_traces: float32 [128, 8192], P(None, 'tm')
Inputs may be any that keep to these rules, and one draw needn't show every extreme that they name: `patch_counts`: some patch holds exactly 16 neurons. `slot_neuron`: every neuron id stands exactly once.
All inputs are finite; a program needn't handle non-finite values.
Results may differ from a plain program's by a relative error of at most 0.0075.
Values sent between devices are 32-bit elements; how exact they have to be, the bound alone decides.
No kernel may reach another device: no remote copies, remote signals or barrier semaphores. Data moves between devices by JAX's collectives and lax.ppermute only.
A program may use at most 64 MiB of HBM per device.

v0:
```python
import jax
import jax.numpy as jnp
from jax import lax
from jax.sharding import PartitionSpec as P

ITERS = 2
SWEEPS = 3


RIDGE = 1.0
HIGH = lax.Precision.HIGHEST


def hals_sweeps(values, target, gram):
    slot_count = values.shape[0]

    def advance(slot_index, current):
        gram_row = lax.dynamic_index_in_dim(gram, slot_index, 1, keepdims=False)
        mixed = jnp.einsum("pt,tpw->pw", gram_row, current, precision=HIGH)
        diagonal_term = lax.dynamic_index_in_dim(gram_row, slot_index, 1, keepdims=False)[:, None]
        own_value = lax.dynamic_index_in_dim(current, slot_index, 0, keepdims=False)
        target_row = lax.dynamic_index_in_dim(target, slot_index, 0, keepdims=False)
        refreshed = jnp.maximum(
            (target_row - mixed + diagonal_term * own_value) / (diagonal_term + RIDGE), 0.0
        )
        return lax.dynamic_update_index_in_dim(current, refreshed, slot_index, 0)

    for sweep_index in range(SWEEPS):
        values = lax.fori_loop(0, slot_count, advance, values)
    return values


def local(movie, footprints, traces, patch_counts, slot_neuron):
    slot_count, patch_total, voxel_share = footprints.shape
    frame_share = movie.shape[2]
    live = (jnp.arange(slot_count, dtype=jnp.int32)[:, None] < patch_counts[None, :]).astype(
        jnp.float32
    )
    shape_a = footprints * live[:, :, None]
    picked = jnp.take(traces, slot_neuron, axis=0)
    shape_c = (
        picked.reshape(patch_total, slot_count, frame_share).transpose(1, 0, 2) * live[:, :, None]
    )
    for outer_index in range(ITERS):
        low_a = shape_a.astype(jnp.bfloat16)
        projected = jnp.einsum("spv,pvf->spf", low_a, movie, preferred_element_type=jnp.float32)
        footprint_gram = jnp.einsum("spv,tpv->pst", shape_a, shape_a, precision=HIGH)
        projected, footprint_gram = lax.psum((projected, footprint_gram), ("tile", "plane"))
        shape_c = hals_sweeps(shape_c, projected, footprint_gram)
        low_c = shape_c.astype(jnp.bfloat16)
        correlated = jnp.einsum("spf,pvf->spv", low_c, movie, preferred_element_type=jnp.float32)
        trace_gram = jnp.einsum("spf,tpf->pst", shape_c, shape_c, precision=HIGH)
        correlated, trace_gram = lax.psum((correlated, trace_gram), "tm")
        shape_a = hals_sweeps(shape_a, correlated, trace_gram)
    flat_c = shape_c.transpose(1, 0, 2).reshape(patch_total * slot_count, frame_share)
    flat_live = live.T.reshape(-1)
    kept = jnp.where(flat_live[:, None] > 0.5, flat_c, picked)
    new_traces = jnp.zeros_like(traces).at[slot_neuron].set(kept)
    return (shape_a, new_traces)


def solution(mesh):
    placed = (
        P(None, ("tile", "plane"), "tm"),
        P(None, None, ("tile", "plane")),
        P(None, "tm"),
        P(),
        P(),
    )
    return jax.shard_map(
        local,
        mesh=mesh,
        in_specs=placed,
        out_specs=(P(None, None, ("tile", "plane")), P(None, "tm")),
        check_vma=False,
    )
```

profile of v0, /device:TPU:8, one launch (start us, length us, event | category | flops | bytes accessed | tf_op | source)
XLA Modules:
  0.0 959.9 jit_solution(8385254858329616595)
XLA Ops:
  10.8 66.9 %psum.57 = f32[8,16,16]{2,1,0:T(8,128)S(1)} all-reduce(f32[8,16,16]{2,1,0:T(8,128)S(1)} %fusion.62), channel_id=1, replica_groups=mesh['tm'=32,'tile'=8,'plane'=2] {'tile','plane'}, use_global_device_ids=true, to_apply=%region_0.1 | all-reduce | flops 2048 | bytes 16384 | tf_op jit(solution)/shard_map/psum | solution.py:48
  78.8 88.6 %all-reduce.5.cloned.1.call-done = f32[16,8,256]{2,0,1:T(8,128)} async-done(((f32[16,8,256]{2,0,1:T(8,128)}), f32[16,8,256]{2,0,1:T(8,128)}) %all-reduce.5.cloned.1.call-update) | async-done | bytes 131088 | tf_op jit(solution)/shard_map/psum | solution.py:48
  168.4 8.4 while.192
  176.9 8.4 while.193
  185.3 8.4 while.194
  193.7 1.4 convolution_bitcast_fusion.1
  195.6 122.4 %psum.59 = f32[8,16,16]{2,1,0:T(8,128)S(1)} all-reduce(f32[8,16,16]{2,1,0:T(8,128)S(1)} %fusion.67), channel_id=1, replica_groups=mesh['tm'=32,'tile'=8,'plane'=2] {'tm'}, use_global_device_ids=true, to_apply=%region_8.9 | all-reduce | flops 2048 | bytes 16384 | tf_op jit(solution)/shard_map/psum | solution.py:53
  318.0 133.7 %all-reduce.7.cloned.1.call-done = f32[16,8,512]{2,0,1:T(8,128)} async-done(((f32[16,8,512]{2,0,1:T(8,128)}), f32[16,8,512]{2,0,1:T(8,128)}) %all-reduce.7.cloned.1.call-update) | async-done | bytes 262160 | tf_op jit(solution)/shard_map/psum | solution.py:53
  451.7 1.1 copy.60
  452.8 11.5 %while.195 = (s32[]{:T(128)}, f32[16,8,512]{2,1,0:T(8,128)S(1)}, f32[16,8,512]{2,1,0:T(8,128)S(1)}, f32[8,16,16]{2,0,1:T(8,128)S(1)}, s32[]{:T(128)}, /*index=5*/s32[]{:T(128)}, s32[]{:T(128)}) while((s32[]{:T(128)}, f32[16,8,512]{2,1,0:T(8,128)S(1)}, f32[16,8,512]{2,1,0:T(8,128)S(1)}, f32[8,16,16]{2,0,1:T(8,128)S(1)}, s32[]{:T(128)}, ...), condition=%wide.region_11.12_spmd, body=%wide.region_10.11_spmd.sunk | while | flops 806923 | bytes 379629 | solution.py:29
  464.3 11.5 %while.196 = (s32[]{:T(128)}, f32[16,8,512]{2,1,0:T(8,128)S(1)}, f32[16,8,512]{2,1,0:T(8,128)S(1)}, f32[8,16,16]{2,0,1:T(8,128)S(1)}, s32[]{:T(128)}, /*index=5*/s32[]{:T(128)}, s32[]{:T(128)}) while((s32[]{:T(128)}, f32[16,8,512]{2,1,0:T(8,128)S(1)}, f32[16,8,512]{2,1,0:T(8,128)S(1)}, f32[8,16,16]{2,0,1:T(8,128)S(1)}, s32[]{:T(128)}, ...), condition=%wide.region_13.14_spmd, body=%wide.region_12.13_spmd.sunk | while | flops 806923 | bytes 379629 | solution.py:29
  475.8 11.5 %while.197 = (s32[]{:T(128)}, f32[16,8,512]{2,1,0:T(8,128)S(1)}, f32[16,8,512]{2,1,0:T(8,128)S(1)}, f32[8,16,16]{2,0,1:T(8,128)S(1)}, s32[]{:T(128)}, /*index=5*/s32[]{:T(128)}, s32[]{:T(128)}) while((s32[]{:T(128)}, f32[16,8,512]{2,1,0:T(8,128)S(1)}, f32[16,8,512]{2,1,0:T(8,128)S(1)}, f32[8,16,16]{2,0,1:T(8,128)S(1)}, s32[]{:T(128)}, ...), condition=%wide.region_15.16_spmd, body=%wide.region_14.15_spmd.sunk | while | flops 806923 | bytes 379629 | solution.py:29
  489.0 63.9 %psum.61 = f32[8,16,16]{2,1,0:T(8,128)S(1)} all-reduce(f32[8,16,16]{2,1,0:T(8,128)S(1)} %fusion.60), channel_id=1, replica_groups=mesh['tm'=32,'tile'=8,'plane'=2] {'tile','plane'}, use_global_device_ids=true, to_apply=%region_16.17 | all-reduce | flops 2048 | bytes 16384 | tf_op jit(solution)/shard_map/psum | solution.py:48
  552.9 79.9 %all-reduce.9.cloned.1.call-done = f32[16,8,256]{2,0,1:T(8,128)} async-done(((f32[16,8,256]{2,0,1:T(8,128)}), f32[16,8,256]{2,0,1:T(8,128)}) %all-reduce.9.cloned.1.call-update) | async-done | bytes 131088 | tf_op jit(solution)/shard_map/psum | solution.py:48
  633.8 8.4 while.198
  642.2 8.4 while.199
  650.6 8.4 while.200
  659.0 1.4 convolution_bitcast_fusion
  660.7 122.4 %psum.63 = f32[8,16,16]{2,1,0:T(8,128)S(1)} all-reduce(f32[8,16,16]{2,1,0:T(8,128)S(1)} %fusion.64), channel_id=1, replica_groups=mesh['tm'=32,'tile'=8,'plane'=2] {'tm'}, use_global_device_ids=true, to_apply=%region_24.25 | all-reduce | flops 2048 | bytes 16384 | tf_op jit(solution)/shard_map/psum | solution.py:53
  783.3 1.6 scatter_custom_fusion
  784.9 132.1 %all-reduce.11.cloned.1.call-done = f32[16,8,512]{2,0,1:T(8,128)} async-done(((f32[16,8,512]{2,0,1:T(8,128)}), f32[16,8,512]{2,0,1:T(8,128)}) %all-reduce.11.cloned.1.call-update) | async-done | bytes 262160 | tf_op jit(solution)/shard_map/psum | solution.py:53
  918.1 11.5 %while.201 = (s32[]{:T(128)}, f32[16,8,512]{2,1,0:T(8,128)S(1)}, f32[16,8,512]{2,1,0:T(8,128)S(1)}, f32[8,16,16]{2,0,1:T(8,128)S(1)}, s32[]{:T(128)}, /*index=5*/s32[]{:T(128)}, s32[]{:T(128)}) while((s32[]{:T(128)}, f32[16,8,512]{2,1,0:T(8,128)S(1)}, f32[16,8,512]{2,1,0:T(8,128)S(1)}, f32[8,16,16]{2,0,1:T(8,128)S(1)}, s32[]{:T(128)}, ...), condition=%wide.region_27.28_spmd, body=%wide.region_26.27_spmd.sunk | while | flops 806923 | bytes 379629 | solution.py:29
  929.6 11.5 %while.202 = (s32[]{:T(128)}, f32[16,8,512]{2,1,0:T(8,128)S(1)}, f32[16,8,512]{2,1,0:T(8,128)S(1)}, f32[8,16,16]{2,0,1:T(8,128)S(1)}, s32[]{:T(128)}, /*index=5*/s32[]{:T(128)}, s32[]{:T(128)}) while((s32[]{:T(128)}, f32[16,8,512]{2,1,0:T(8,128)S(1)}, f32[16,8,512]{2,1,0:T(8,128)S(1)}, f32[8,16,16]{2,0,1:T(8,128)S(1)}, s32[]{:T(128)}, ...), condition=%wide.region_29.30_spmd, body=%wide.region_28.29_spmd.sunk | while | flops 806923 | bytes 379629 | solution.py:29
  941.1 11.5 %while.203 = (s32[]{:T(128)}, f32[16,8,512]{2,1,0:T(8,128)S(1)}, f32[16,8,512]{2,1,0:T(8,128)S(1)}, f32[8,16,16]{2,0,1:T(8,128)S(1)}, s32[]{:T(128)}, /*index=5*/s32[]{:T(128)}, s32[]{:T(128)}) while((s32[]{:T(128)}, f32[16,8,512]{2,1,0:T(8,128)S(1)}, f32[16,8,512]{2,1,0:T(8,128)S(1)}, f32[8,16,16]{2,0,1:T(8,128)S(1)}, s32[]{:T(128)}, ...), condition=%wide.region_31.32_spmd, body=%wide.region_30.31_spmd.sunk | while | flops 806923 | bytes 379629 | solution.py:29
  (1199 shorter events, 126.3 us)
Async XLA Ops:
  7.2 1.9 copy-start
  7.2 3.1 copy-start.4
  7.2 70.8 %copy-start.2 = (f32[128,256]{1,0:T(8,128)S(1)}, f32[128,256]{1,0:T(8,128)}, u32[]{:S(2)}) copy-start(f32[128,256]{1,0:T(8,128)} %param.31) | copy-start | bytes 393220
  7.2 160.3 %all-reduce.5.cloned.1.call-start = ((), (), s32[]{:S(2)}) async-start(), calls=%async_computation | async-start | bytes 262144 | tf_op jit(solution)/shard_map/psum | solution.py:48
  10.2 441.5 %all-reduce.7.cloned.1.call-start = ((), (), s32[]{:S(2)}) async-start(), calls=%async_computation.1 | async-start | bytes 524288 | tf_op jit(solution)/shard_map/psum | solution.py:53
  185.3 9.8 %copy-start.3 = (s32[8]{0:T(128)S(1)}, s32[8]{0:T(128)}, u32[]{:S(2)}) copy-start(s32[8]{0:T(128)} %param.32) | copy-start | bytes 100
  195.1 437.8 %all-reduce.9.cloned.1.call-start = ((), (), s32[]{:S(2)}) async-start(), calls=%async_computation.2 | async-start | bytes 262144 | tf_op jit(solution)/shard_map/psum | solution.py:48
  488.4 428.6 %all-reduce.11.cloned.1.call-start = ((), (), s32[]{:S(2)}) async-start(), calls=%async_computation.3 | async-start | bytes 524288 | tf_op jit(solution)/shard_map/psum | solution.py:53
  952.6 0.7 copy-start.1
Sparse Core Ops, SparseCore 0:
  11.5 155.9 all-reduce.4
  195.2 256.4 all-reduce.6
  488.5 144.2 all-reduce.8
  660.5 256.4 all-reduce.10
where the time goes:
time: 960 us
  waiting for transfers between devices  434 us (45%)
  blocking collectives  376 us (39%)
  matrix products  67.5 us (7%)
  local copies, waits for them, and re-layouts  45.2 us (5%)
  other arithmetic  18.8 us (2%)
  between operations  13.9 us (1%)
    psum x2, waiting for transfers between devices, local(): correlated, trace_gram = lax.psum((correlated, trace_gram), 'tm')  266 us
    psum x2, blocking collectives, local(): correlated, trace_gram = lax.psum((correlated, trace_gram), 'tm')  245 us
    psum x2, waiting for transfers between devices, local(): lax.psum((projected, footprint_gram), ('tile', 'plane'))  169 us
    psum x2, blocking collectives, local(): lax.psum((projected, footprint_gram), ('tile', 'plane'))  131 us
    dot_general x192, matrix products, advance(): mixed = jnp.einsum('pt,tpw->pw', gram_row, current, precision=HIGH)  61 us
    dynamic_slice x192, local copies, waits for them, and re-layouts, advance(): lax.dynamic_index_in_dim(gram_row, slot_index, 1, keepdims=False)[:, None]  35.8 us
  transfers between devices with their start and end apart: 4, of which 4 were waited for; matrix products, arithmetic and copies ran while one was open for 0% of the time, Pallas kernels for 0%

commit v1 on v0

v1 whole, which is shorter than its diff:
```python
import functools

import jax
import jax.numpy as jnp
from jax import lax
from jax.experimental import pallas as pl
from jax.experimental.pallas import tpu as pltpu
from jax.sharding import PartitionSpec as P

ITERS = 2
SWEEPS = 3
RIDGE = 1.0
HIGH = lax.Precision.HIGHEST
F32 = jnp.float32
BF16 = jnp.bfloat16
KP = 16
NP = 8
LIVE = 64
VOX = ("tile", "plane")

SMEM = pl.BlockSpec(memory_space=pltpu.SMEM)
VMEM = pl.BlockSpec(memory_space=pltpu.VMEM)


def nn(a, b, **kw):
    return lax.dot_general(a, b, (((1,), (0,)), ((), ())), preferred_element_type=F32, **kw)


def nt(a, b, **kw):
    return lax.dot_general(a, b, (((1,), (1,)), ((), ())), preferred_element_type=F32, **kw)


def offsets(counts):
    offs = [jnp.int32(0)]
    for p in range(NP):
        offs.append(offs[-1] + counts[p])
    return offs


def iota(shape, dim):
    return lax.broadcasted_iota(jnp.int32, shape, dim)


def patch_and_slot(counts, shape, dim):
    offs = offsets(counts)
    r = iota(shape, dim)
    patch = jnp.zeros(shape, jnp.int32)
    slot = r
    for p in range(1, NP):
        at = r >= offs[p]
        patch = jnp.where(at, p, patch)
        slot = jnp.where(at, r - offs[p], slot)
    return patch, slot


def unpacker(counts):
    offs = offsets(counts)
    shape = (KP * NP, LIVE)
    q, r = iota(shape, 0), iota(shape, 1)
    p, s = q % NP, q // NP
    off = jnp.zeros(shape, jnp.int32)
    cnt = jnp.zeros(shape, jnp.int32)
    for i in range(NP):
        off = jnp.where(p == i, offs[i], off)
        cnt = jnp.where(p == i, counts[i], cnt)
    return ((r == off + s) & (s < cnt)).astype(F32)


def packer(counts):
    shape = (LIVE, KP * NP)
    patch, slot = patch_and_slot(counts, shape, 0)
    return (iota(shape, 1) == slot * NP + patch).astype(F32)


def gram_chunk(counts, full):
    shape = (LIVE, LIVE)
    patch_a, _ = patch_and_slot(counts, shape, 0)
    patch_b, _ = patch_and_slot(counts, shape, 1)
    own = jnp.where(patch_a == patch_b, full, 0.0)
    _, slot = patch_and_slot(counts, (KP, LIVE), 1)
    pick = (slot == iota((KP, LIVE), 0)).astype(F32)
    by_slot = nn(pick, own, precision=HIGH)
    return jnp.concatenate([by_slot[:8], by_slot[8:]], axis=1)


def project_packed(counts, packed, movie_ref, send_ref):
    low = packed.astype(BF16)
    patch, _ = patch_and_slot(counts, low.shape, 0)
    zero = jnp.zeros_like(low)
    total = jnp.zeros((LIVE, movie_ref.shape[2]), F32)
    for p in range(NP):
        total += nn(jnp.where(patch == p, low, zero), movie_ref[p])
    gram = gram_chunk(counts, nt(packed, packed, precision=HIGH))
    stacked = jnp.concatenate([total[:, :128], total[:, 128:]], axis=0)
    chunks = stacked.T
    for j in range(send_ref.shape[0]):
        send_ref[j, 0:8, :] = chunks[8 * j : 8 * j + 8]
        send_ref[j, 8:16, :] = gram


def first_project_kernel(counts, foot_ref, movie_ref, send_ref):
    packed = nn(packer(counts), foot_ref[...], precision=HIGH)
    project_packed(counts, packed, movie_ref, send_ref)


def project_kernel(counts, gathered_ref, movie_ref, send_ref):
    rows = jnp.concatenate([gathered_ref[:128].T, gathered_ref[128:].T], axis=1)
    packed = jnp.concatenate([rows[:LIVE], rows[LIVE:]], axis=1)
    project_packed(counts, packed, movie_ref, send_ref)


def correlate_kernel(counts, gathered_ref, movie_ref, send_ref):
    by_frame = gathered_ref[...]
    rows = by_frame.T
    cols = jnp.concatenate([by_frame[:, :LIVE], by_frame[:, LIVE:]], axis=0)
    gram = gram_chunk(
        counts,
        nt(rows[:LIVE], rows[:LIVE], precision=HIGH) + nt(rows[LIVE:], rows[LIVE:], precision=HIGH),
    )
    low = cols.astype(BF16)
    patch, _ = patch_and_slot(counts, low.shape, 1)
    zero = jnp.zeros_like(low)
    total = jnp.zeros((movie_ref.shape[1], LIVE), F32)
    for p in range(NP):
        total += nn(movie_ref[p], jnp.where(patch == p, low, zero))
    half = total.shape[0] // 2
    chunks = jnp.concatenate([total[:half], total[half:]], axis=1)
    for i in range(send_ref.shape[0]):
        send_ref[i, 0:8, :] = chunks[8 * i : 8 * i + 8]
        send_ref[i, 8:16, :] = gram


def own_columns(ref, index, lanes):
    base = pl.multiple_of((index // 16) * 128, 128)
    turn = 8 * (index % 16)
    low = pltpu.roll(ref[:, pl.ds(base, 128)], (128 - turn) % 128, 1)
    high = pltpu.roll(ref[:, pl.ds(lanes + base, 128)], (136 - turn) % 128, 1)
    return jnp.where(iota(low.shape, 1) < 8, low, high)


def start_kernel(counts, where, foot_ref, traces_ref, choose_ref, first_c_ref, first_a_ref):
    q = iota((KP * NP, 128), 0)
    cnt = jnp.zeros(q.shape, jnp.int32)
    for p in range(NP):
        cnt = jnp.where(q % NP == p, counts[p], cnt)
    live = q // NP < cnt
    keep = live & (iota(q.shape, 1) < 16)
    first_a = own_columns(foot_ref, where[0], foot_ref.shape[1] // 2)
    first_a_ref[...] = jnp.where(keep, first_a, 0.0)
    traces = own_columns(traces_ref, where[1], traces_ref.shape[1] // 2)
    first_c_ref[...] = jnp.where(keep, nn(choose_ref[...], traces, precision=HIGH), 0.0)


def hals_kernel(counts, got_ref, x_ref, send_ref, new_ref, rows, wide):
    n = got_ref.shape[0]
    parts = [got_ref[j] for j in range(n)]
    while len(parts) > 1:
        parts = [a + b for a, b in zip(parts[::2], parts[1::2])]
    total = parts[0]
    cols = jnp.concatenate([total[:, :LIVE], total[:, LIVE:]], axis=0)
    order = jnp.concatenate([cols[0:8], cols[16:24], cols[8:16], cols[24:32]], axis=0)
    unpack = unpacker(counts)
    rows[:, 0:32] = nt(unpack, order, precision=HIGH)
    shape = (NP, 128)
    scale = []
    for k in range(KP):
        own = rows[8 * k : 8 * k + 8, :]
        for t in range(KP):
            entry = jnp.broadcast_to(own[:, 16 + t : 17 + t], shape)
            if t == k:
                scale.append(1.0 / (entry + RIDGE))
            wide[KP * k + t] = entry
    for k in range(KP):
        wide[KP * k + k] = scale[k]

    def sweep(_, xs):
        xs = list(xs)
        for k in range(KP):
            terms = [wide[KP * k + t] * xs[t] for t in range(KP) if t != k]
            last = terms.pop(k - 1 if k else KP - 2)
            while len(terms) > 1:
                odd = [terms[-1]] if len(terms) % 2 else []
                terms = [a + b for a, b in zip(terms[::2], terms[1::2])] + odd
            rest = rows[8 * k : 8 * k + 8, :] - terms[0]
            xs[k] = jnp.maximum((rest - last) * wide[KP * k + k], 0.0)
        return tuple(xs)

    keep = iota(shape, 1) < 16
    xs = lax.fori_loop(0, SWEEPS, sweep, tuple(x_ref[8 * k : 8 * k + 8, :] for k in range(KP)))
    for k in range(KP):
        new_ref[8 * k : 8 * k + 8, :] = jnp.where(keep, xs[k], 0.0)
    by_col = new_ref[...].T[:16]
    packed = nn(by_col, unpack, precision=HIGH)
    chunk = jnp.concatenate([packed[:8], packed[8:]], axis=1)
    for j in range(n):
        send_ref[j] = chunk


def footprints_kernel(counts, gathered_ref, out_ref):
    half = gathered_ref.shape[0]
    unpack = unpacker(counts)
    gathered = gathered_ref[...]
    out_ref[:, :half] = nt(unpack, gathered[:, :LIVE], precision=HIGH)
    out_ref[:, half:] = nt(unpack, gathered[:, LIVE:], precision=HIGH)


def traces_kernel(counts, gathered_ref, traces_ref, home_ref, out_ref):
    half = gathered_ref.shape[0]
    gathered = gathered_ref[...]
    home = home_ref[...]
    place = nn(home, unpacker(counts), precision=HIGH)
    live = jnp.sum(home, axis=1, keepdims=True) > 0.5
    for h in range(2):
        at = slice(half * h, half * h + half)
        moved = nt(place, gathered[:, LIVE * h : LIVE * h + LIVE], precision=HIGH)
        out_ref[:, at] = jnp.where(live, moved, traces_ref[:, at])


def call(kernel, outs, smem, args, scratch=()):
    return pl.pallas_call(
        kernel,
        out_shape=[jax.ShapeDtypeStruct(s, F32) for s in outs],
        in_specs=[SMEM] * smem + [VMEM] * (len(args) - smem),
        out_specs=[VMEM] * len(outs),
        scratch_shapes=list(scratch),
        compiler_params=pltpu.CompilerParams(vmem_limit_bytes=32 * 1024 * 1024),
    )(*args)


def local(n_tm, n_vox, movie, footprints, traces, patch_counts, slot_neuron):
    slots, patches, voxels = footprints.shape
    frames = movie.shape[2]
    q = slots * patches
    foot = footprints.reshape(q, voxels)
    neuron = slot_neuron.reshape(patches, slots).T.reshape(q)
    live = (jnp.arange(slots, dtype=jnp.int32)[:, None] < patch_counts[None, :]).reshape(q)
    ids = jnp.arange(q, dtype=jnp.int32)
    choose = ((neuron[:, None] == ids[None, :]) & live[:, None]).astype(F32)
    home = ((neuron[None, :] == ids[:, None]) & live[None, :]).astype(F32)
    where = jnp.stack([lax.axis_index("tm"), lax.axis_index(VOX)]).astype(jnp.int32)

    def swap(x, axes):
        return lax.all_to_all(x, axes, 0, 0, tiled=True)

    def hals(n, got, x):
        scratch = [pltpu.VMEM((q, 128), F32), pltpu.VMEM((KP * KP, NP, 128), F32)]
        return call(hals_kernel, [(n, 8, 128), (q, 128)], 1, [patch_counts, got, x], scratch)

    chunk_c = (n_vox, 16, 128)
    chunk_a = (n_tm, 16, 128)
    x_c, x_a = call(start_kernel, [(q, 128)] * 2, 2, [patch_counts, where, foot, traces, choose])
    for step in range(ITERS):
        if step == 0:
            (send,) = call(first_project_kernel, [chunk_c], 1, [patch_counts, foot, movie])
        else:
            (send,) = call(project_kernel, [chunk_c], 1, [patch_counts, all_a, movie])
        send, x_c = hals(n_vox, swap(send, VOX), x_c)
        all_c = swap(send, VOX).reshape(frames // 2, 128)
        (send,) = call(correlate_kernel, [chunk_a], 1, [patch_counts, all_c, movie])
        send, x_a = hals(n_tm, swap(send, "tm"), x_a)
        all_a = swap(send, "tm").reshape(voxels // 2, 128)
    (new_traces,) = call(traces_kernel, [traces.shape], 1, [patch_counts, all_c, traces, home])
    (new_foot,) = call(footprints_kernel, [foot.shape], 1, [patch_counts, all_a])
    return new_foot.reshape(footprints.shape), new_traces


def solution(mesh):
    placed = (
        P(None, ("tile", "plane"), "tm"),
        P(None, None, ("tile", "plane")),
        P(None, "tm"),
        P(),
        P(),
    )
    n_tm = mesh.shape["tm"]
    n_vox = mesh.shape["tile"] * mesh.shape["plane"]
    return jax.shard_map(
        functools.partial(local, n_tm, n_vox),
        mesh=mesh,
        in_specs=placed,
        out_specs=(P(None, None, ("tile", "plane")), P(None, "tm")),
        check_vma=False,
    )
```

time: 960 us -> 171 us (0.18)
  waiting for transfers between devices: 434 us -> 19.6 us
  blocking collectives: 376 us -> 113 us
  matrix products: 67.5 us -> 0 us
  local copies, waits for them, and re-layouts: 45.2 us -> 3.56 us
  Pallas kernels: 0 us -> 20.4 us
  other arithmetic: 18.8 us -> 0.19 us
  between operations: 13.9 us -> 0.74 us
  starting transfers between devices: 0.16 us -> 13 us
    psum x4 -> x0, waiting for transfers between devices: 434 us -> none  [the longest x2 266 us: local(): correlated, trace_gram = lax.psum((correlated, trace_gram), 'tm')]
    psum x4 -> x0, blocking collectives: 376 us -> none  [the longest x2 245 us: local(): correlated, trace_gram = lax.psum((correlated, trace_gram), 'tm')]
    all_to_all x0 -> x6, blocking collectives: none -> 113 us  [swap(): return lax.all_to_all(x, axes, 0, 0, tiled=True)]
    dot_general x200 -> x0, matrix products: 67.5 us -> none  [the longest x192 61 us: advance(): mixed = jnp.einsum('pt,tpw->pw', gram_row, current, precision=HIGH)]
    dynamic_slice x576 -> x0, local copies, waits for them, and re-layouts: 37.5 us -> none  [the longest x192 35.8 us: advance(): lax.dynamic_index_in_dim(gram_row, slot_index, 1, keepdims=False)[:, None]]
    pallas_call x0 -> x11, Pallas kernels: none -> 20.4 us  [call(): pl.pallas_call(kernel, out_shape=[jax.ShapeDtypeStruct(s, F32) for s in o...]
    all_to_all x0 -> x2, waiting for transfers between devices: none -> 19.6 us  [swap(): return lax.all_to_all(x, axes, 0, 0, tiled=True)]
    dynamic_update_slice x192 -> x0, other arithmetic: 15.4 us -> none  [advance(): return lax.dynamic_update_index_in_dim(current, refreshed, slot_index, 0)]
  transfers between devices with their start and end apart: 4 -> 2, of which waited for: 4 -> 2; matrix products, arithmetic and copies ran while one was open for 0% -> 0% of each run, Pallas kernels for 0% -> 2%
where the time goes in v1:
time: 171 us
  blocking collectives  113 us (66%)
  Pallas kernels  20.4 us (12%)
  waiting for transfers between devices  19.6 us (11%)
  starting transfers between devices  13 us (8%)
  local copies, waits for them, and re-layouts  3.56 us (2%)
    all_to_all x6, blocking collectives, swap(): return lax.all_to_all(x, axes, 0, 0, tiled=True)  113 us
    pallas_call x11, Pallas kernels, call(): pl.pallas_call(kernel, out_shape=[jax.ShapeDtypeStruct(s, F32) for s in o...  20.4 us
    all_to_all x2, waiting for transfers between devices, swap(): return lax.all_to_all(x, axes, 0, 0, tiled=True)  19.6 us
    all_to_all x2, starting transfers between devices, swap(): return lax.all_to_all(x, axes, 0, 0, tiled=True)  13 us
  transfers between devices with their start and end apart: 2, of which 2 were waited for; matrix products, arithmetic and copies ran while one was open for 0% of the time, Pallas kernels for 2%

profile of v1, /device:TPU:8, one launch (start us, length us, event | category | flops | bytes accessed | tf_op | source)
XLA Modules:
  0.0 170.5 jit_solution(17791330651107947189)
XLA Ops:
  0.7 1.6 copy-done
  2.3 0.9 copy-done.2
  3.2 0.7 copy-done.5
  3.9 2.2 %shard_map.68 = f32[16,16,128]{2,1,0:T(8,128)} custom-call(s32[8]{0:T(128)S(1)} %copy-done.5, f32[128,512]{1,0:T(8,128)S(1)} %bitcast.9, bf16[8,512,256]{2,1,0:T(8,128)(2,1)S(1)} %copy-done), custom_call_target="tpu_custom_call" | custom-call | tf_op jit(solution)/shard_map/pallas_call | solution.py:220
  6.1 9.1 %all-to-all-start = ((f32[16,16,128]{2,1,0:T(8,128)}), f32[16,16,128]{2,1,0:T(8,128)S(1)}, u32[]{:S(2)}, u32[]{:S(2)}) async-start(f32[16,16,128]{2,1,0:T(8,128)} %shard_map.68), calls=%async_computation | async-start | bytes 262144 | tf_op jit(solution)/shard_map/all_to_all | solution.py:243
  15.8 0.8 shard_map.69
  16.7 5.4 %all-to-all-done.got_ref = f32[16,16,128]{2,1,0:T(8,128)S(1)} async-done(((f32[16,16,128]{2,1,0:T(8,128)}), f32[16,16,128]{2,1,0:T(8,128)S(1)}, u32[]{:S(2)}, u32[]{:S(2)}) %all-to-all-start) | async-done | bytes 131104 | tf_op jit(solution)/shard_map/all_to_all | solution.py:243
  22.1 1.9 %shard_map.70 = (f32[16,8,128]{2,1,0:T(8,128)S(1)}, f32[128,128]{1,0:T(8,128)S(1)}) custom-call(s32[8]{0:T(128)S(1)} %copy-done.6, f32[16,16,128]{2,1,0:T(8,128)S(1)} %all-to-all-done.got_ref, f32[128,128]{1,0:T(8,128)S(1)} %get-tuple-element.10.x_ref), custom_call_target="tpu_custom_call" | custom-call | tf_op jit(solution)/shard_map/pallas_call | solution.py:220
  24.0 10.4 %all_to_all.40 = f32[16,8,128]{2,1,0:T(8,128)S(1)} all-to-all(f32[16,8,128]{2,1,0:T(8,128)S(1)} %get-tuple-element.11), channel_id=1, replica_groups=mesh['tm'=32,'tile'=8,'plane'=2] {'tile','plane'}, dimensions={0} | all-to-all | bytes 131072 | tf_op jit(solution)/shard_map/all_to_all | solution.py:243
  34.3 1.8 %shard_map.71 = f32[32,16,128]{2,1,0:T(8,128)S(1)} custom-call(s32[8]{0:T(128)S(1)} %copy-done.6, f32[128,128]{1,0:T(8,128)S(1)} %bitcast.15, bf16[8,512,256]{2,1,0:T(8,128)(2,1)S(1)} %copy-done.1), custom_call_target="tpu_custom_call" | custom-call | tf_op jit(solution)/shard_map/pallas_call | solution.py:220
  36.2 36.0 %all_to_all.41.got_ref = f32[32,16,128]{2,1,0:T(8,128)S(1)} all-to-all(f32[32,16,128]{2,1,0:T(8,128)S(1)} %shard_map.71), channel_id=1, replica_groups=mesh['tm'=32,'tile'=8,'plane'=2] {'tm'}, dimensions={0} | all-to-all | bytes 524288 | tf_op jit(solution)/shard_map/all_to_all | solution.py:243
  72.1 1.9 %shard_map.72 = (f32[32,8,128]{2,1,0:T(8,128)S(1)}, f32[128,128]{1,0:T(8,128)S(1)}) custom-call(s32[8]{0:T(128)S(1)} %copy-done.6, f32[32,16,128]{2,1,0:T(8,128)S(1)} %all_to_all.41.got_ref, f32[128,128]{1,0:T(8,128)S(1)} %get-tuple-element.12.x_ref), custom_call_target="tpu_custom_call" | custom-call | tf_op jit(solution)/shard_map/pallas_call | solution.py:220
  74.1 19.5 %all_to_all.42 = f32[32,8,128]{2,1,0:T(8,128)S(1)} all-to-all(f32[32,8,128]{2,1,0:T(8,128)S(1)} %get-tuple-element.13), channel_id=1, replica_groups=mesh['tm'=32,'tile'=8,'plane'=2] {'tm'}, dimensions={0} | all-to-all | bytes 262144 | tf_op jit(solution)/shard_map/all_to_all | solution.py:243
  93.6 1.3 shard_map.73
  94.9 11.2 %all_to_all.43.got_ref = f32[16,16,128]{2,1,0:T(8,128)S(1)} all-to-all(f32[16,16,128]{2,1,0:T(8,128)S(1)} %shard_map.73), channel_id=1, replica_groups=mesh['tm'=32,'tile'=8,'plane'=2] {'tile','plane'}, dimensions={0} | all-to-all | bytes 262144 | tf_op jit(solution)/shard_map/all_to_all | solution.py:243
  106.1 2.2 %shard_map.74 = (f32[16,8,128]{2,1,0:T(8,128)S(1)}, f32[128,128]{1,0:T(8,128)}) custom-call(s32[8]{0:T(128)S(1)} %copy-done.6, f32[16,16,128]{2,1,0:T(8,128)S(1)} %all_to_all.43.got_ref, f32[128,128]{1,0:T(8,128)S(1)} %get-tuple-element.14.x_ref), custom_call_target="tpu_custom_call" | custom-call | tf_op jit(solution)/shard_map/pallas_call | solution.py:220
  108.3 10.4 %all_to_all.44 = f32[16,8,128]{2,1,0:T(8,128)S(1)} all-to-all(f32[16,8,128]{2,1,0:T(8,128)S(1)} %get-tuple-element.15), channel_id=1, replica_groups=mesh['tm'=32,'tile'=8,'plane'=2] {'tile','plane'}, dimensions={0} | all-to-all | bytes 131072 | tf_op jit(solution)/shard_map/all_to_all | solution.py:243
  118.7 1.8 %shard_map.75 = f32[32,16,128]{2,1,0:T(8,128)S(1)} custom-call(s32[8]{0:T(128)S(1)} %copy-done.6, f32[128,128]{1,0:T(8,128)S(1)} %bitcast.11, bf16[8,512,256]{2,1,0:T(8,128)(2,1)S(1)} %copy-done.1), custom_call_target="tpu_custom_call" | custom-call | tf_op jit(solution)/shard_map/pallas_call | solution.py:220
  120.5 25.7 %all_to_all.45.got_ref = f32[32,16,128]{2,1,0:T(8,128)S(1)} all-to-all(f32[32,16,128]{2,1,0:T(8,128)S(1)} %shard_map.75), channel_id=1, replica_groups=mesh['tm'=32,'tile'=8,'plane'=2] {'tm'}, dimensions={0} | all-to-all | bytes 524288 | tf_op jit(solution)/shard_map/all_to_all | solution.py:243
  146.2 2.6 %shard_map.76 = (f32[32,8,128]{2,1,0:T(8,128)}, f32[128,128]{1,0:T(8,128)}) custom-call(s32[8]{0:T(128)S(1)} %copy-done.6, f32[32,16,128]{2,1,0:T(8,128)S(1)} %all_to_all.45.got_ref, f32[128,128]{1,0:T(8,128)S(1)} %get-tuple-element.16.x_ref), custom_call_target="tpu_custom_call" | custom-call | tf_op jit(solution)/shard_map/pallas_call | solution.py:220
  148.8 3.9 %all-to-all-start.7 = ((f32[32,8,128]{2,1,0:T(8,128)}), f32[32,8,128]{2,1,0:T(8,128)S(1)}, u32[]{:S(2)}, u32[]{:S(2)}) async-start(f32[32,8,128]{2,1,0:T(8,128)} %get-tuple-element.17), calls=%async_computation.7 | async-start | bytes 262144 | tf_op jit(solution)/shard_map/all_to_all | solution.py:243
  152.7 1.9 %shard_map.78 = f32[128,256]{1,0:T(8,128)} custom-call(s32[8]{0:T(128)S(1)} %copy-done.6, f32[128,128]{1,0:T(8,128)S(1)} %bitcast.12, f32[128,256]{1,0:T(8,128)S(1)} %copy-done.4, f32[128,128]{1,0:T(8,128)S(1)} %get-tuple-element.18.home_ref), custom_call_target="tpu_custom_call" | custom-call | tf_op jit(solution)/shard_map/pallas_call | solution.py:220
  154.6 14.2 %all-to-all-done.7 = f32[32,8,128]{2,1,0:T(8,128)S(1)} async-done(((f32[32,8,128]{2,1,0:T(8,128)}), f32[32,8,128]{2,1,0:T(8,128)S(1)}, u32[]{:S(2)}, u32[]{:S(2)}) %all-to-all-start.7) | async-done | bytes 131104 | tf_op jit(solution)/shard_map/all_to_all | solution.py:243
  168.8 1.7 shard_map.77
  (20 shorter events, 0.5 us)
Async XLA Ops:
  0.6 14.6 %copy-start.6 = (s32[8]{0:T(128)S(1)}, s32[8]{0:T(128)}, u32[]{:S(2)}) copy-start(s32[8]{0:T(128)} %counts.21) | copy-start | bytes 100
  0.6 14.7 %copy-start.7 = (s32[128]{0:T(128)S(1)}, s32[128]{0:T(128)}, u32[]{:S(2)}) copy-start(s32[128]{0:T(128)} %param.9) | copy-start | bytes 1540
  0.7 1.6 copy-start
  2.3 0.9 copy-start.2
  3.2 0.7 copy-start.5
  3.9 12.0 %copy-start.3 = (f32[16,8,512]{2,1,0:T(8,128)S(1)}, f32[16,8,512]{2,1,0:T(8,128)}, u32[]{:S(2)}) copy-start(f32[16,8,512]{2,1,0:T(8,128)} %param.6) | copy-start | bytes 786436
  3.9 12.0 %copy-start.4 = (f32[128,256]{1,0:T(8,128)S(1)}, f32[128,256]{1,0:T(8,128)}, u32[]{:S(2)}) copy-start(f32[128,256]{1,0:T(8,128)} %traces_ref.3) | copy-start | bytes 393220
  3.9 30.5 %copy-start.1 = (bf16[8,512,256]{2,1,0:T(8,128)(2,1)S(1)}, bf16[8,512,256]{2,1,0:T(8,128)(2,1)}, u32[]{:S(2)}) copy-start(bf16[8,512,256]{2,1,0:T(8,128)(2,1)} %movie_ref.7) | copy-start | bytes 6291460
  6.1 15.9 %all-to-all-start = ((f32[16,16,128]{2,1,0:T(8,128)}), f32[16,16,128]{2,1,0:T(8,128)S(1)}, u32[]{:S(2)}, u32[]{:S(2)}) async-start(f32[16,16,128]{2,1,0:T(8,128)} %shard_map.68), calls=%async_computation | async-start | bytes 262144 | tf_op jit(solution)/shard_map/all_to_all | solution.py:243
  148.8 20.0 %all-to-all-start.7 = ((f32[32,8,128]{2,1,0:T(8,128)}), f32[32,8,128]{2,1,0:T(8,128)S(1)}, u32[]{:S(2)}, u32[]{:S(2)}) async-start(f32[32,8,128]{2,1,0:T(8,128)} %get-tuple-element.17), calls=%async_computation.7 | async-start | bytes 262144 | tf_op jit(solution)/shard_map/all_to_all | solution.py:243

commit v2 on v1

v2 whole, which is shorter than its diff:
```python
import functools

import jax
import jax.numpy as jnp
from jax import lax
from jax.experimental import pallas as pl
from jax.experimental.pallas import tpu as pltpu
from jax.sharding import PartitionSpec as P

ITERS = 2
SWEEPS = 3
RIDGE = 1.0
HIGH = lax.Precision.HIGHEST
F32 = jnp.float32
BF16 = jnp.bfloat16
KP = 16
NP = 8
LIVE = 64
ACROSS = ("y", "plane")
NEAR = ("x", "zn")
FAR = "zf"
GRAM = 8

SMEM = pl.BlockSpec(memory_space=pltpu.SMEM)
VMEM = pl.BlockSpec(memory_space=pltpu.VMEM)
HBM = pl.BlockSpec(memory_space=pltpu.HBM)


def nn(a, b, **kw):
    return lax.dot_general(a, b, (((1,), (0,)), ((), ())), preferred_element_type=F32, **kw)


def nt(a, b, **kw):
    return lax.dot_general(a, b, (((1,), (1,)), ((), ())), preferred_element_type=F32, **kw)


def offsets(counts):
    offs = [jnp.int32(0)]
    for p in range(NP):
        offs.append(offs[-1] + counts[p])
    return offs


def iota(shape, dim):
    return lax.broadcasted_iota(jnp.int32, shape, dim)


def patch_and_slot(counts, shape, dim):
    offs = offsets(counts)
    r = iota(shape, dim)
    patch = jnp.zeros(shape, jnp.int32)
    slot = r
    for p in range(1, NP):
        at = r >= offs[p]
        patch = jnp.where(at, p, patch)
        slot = jnp.where(at, r - offs[p], slot)
    return patch, slot


def unpacker(counts):
    offs = offsets(counts)
    shape = (KP * NP, LIVE)
    q, r = iota(shape, 0), iota(shape, 1)
    p, s = q % NP, q // NP
    off = jnp.zeros(shape, jnp.int32)
    cnt = jnp.zeros(shape, jnp.int32)
    for i in range(NP):
        off = jnp.where(p == i, offs[i], off)
        cnt = jnp.where(p == i, counts[i], cnt)
    return ((r == off + s) & (s < cnt)).astype(F32)


def packer(counts):
    shape = (LIVE, KP * NP)
    patch, slot = patch_and_slot(counts, shape, 0)
    return (iota(shape, 1) == slot * NP + patch).astype(F32)


def gram_chunk(counts, full):
    shape = (LIVE, LIVE)
    patch_a, _ = patch_and_slot(counts, shape, 0)
    patch_b, _ = patch_and_slot(counts, shape, 1)
    own = jnp.where(patch_a == patch_b, full, 0.0)
    _, slot = patch_and_slot(counts, (KP, LIVE), 1)
    pick = (slot == iota((KP, LIVE), 0)).astype(F32)
    by_slot = nn(pick, own, precision=HIGH)
    return jnp.concatenate([by_slot[:8], by_slot[8:]], axis=1)


def project_packed(counts, packed, movie, out_ref):
    low = packed.astype(BF16)
    patch, _ = patch_and_slot(counts, low.shape, 0)
    zero = jnp.zeros_like(low)
    total = None
    for p in range(NP):
        term = nn(jnp.where(patch == p, low, zero), movie(p))
        total = term if p == 0 else total + term
    gram = gram_chunk(counts, nt(packed, packed, precision=HIGH))
    for h in range(2):
        out_ref[h, :LIVE, :] = total[:, 128 * h : 128 * h + 128]
        out_ref[h, LIVE:, :] = gram


def first_project_kernel(counts, foot_ref, movie_ref, out_ref, movie_buf, foot_buf, sems):
    copies = [pltpu.make_async_copy(foot_ref, foot_buf, sems.at[NP])]
    for p in range(NP):
        copies.append(pltpu.make_async_copy(movie_ref.at[p], movie_buf.at[p], sems.at[p]))
    for copy in copies:
        copy.start()
    copies[0].wait()
    packed = nn(packer(counts), foot_buf[...], precision=HIGH)

    def movie(p):
        copies[p + 1].wait()
        return movie_buf[p]

    project_packed(counts, packed, movie, out_ref)


def project_kernel(counts, gathered_ref, movie_ref, out_ref):
    rows = jnp.concatenate([gathered_ref[:128].T, gathered_ref[128:].T], axis=1)
    packed = jnp.concatenate([rows[:LIVE], rows[LIVE:]], axis=1)
    project_packed(counts, packed, lambda p: movie_ref[p], out_ref)


def keep_half_kernel(where, got_ref, send_ref):
    kept = got_ref[0, where[0]] + got_ref[1, where[0]]
    for j in range(send_ref.shape[0]):
        send_ref[j] = kept


def keep_part_kernel(got_ref, send_ref):
    total = tree_sum([got_ref[j] for j in range(got_ref.shape[0])])
    for j in range(send_ref.shape[0]):
        send_ref[j] = total


def correlate_kernel(counts, gathered_ref, movie_ref, send_ref):
    rows = jnp.concatenate([gathered_ref[0], gathered_ref[1]], axis=1)
    gram = gram_chunk(counts, nt(rows, rows, precision=HIGH))
    low = rows.T.astype(BF16)
    patch, _ = patch_and_slot(counts, low.shape, 1)
    zero = jnp.zeros_like(low)
    total = None
    for p in range(NP):
        term = nn(movie_ref[p], jnp.where(patch == p, low, zero))
        total = term if p == 0 else total + term
    half = total.shape[0] // 2
    chunks = jnp.concatenate([total[:half], total[half:]], axis=1)
    n = send_ref.shape[0]
    size = half // n
    for i in range(n):
        send_ref[i, :size, :] = chunks[size * i : size * i + size]
        send_ref[i, size:, :] = gram


def start_kernel(counts, where, foot_ref, traces_ref, choose_ref, first_c_ref, first_a_ref):
    q = iota((KP * NP, 128), 0)
    lane = iota(q.shape, 1)
    cnt = jnp.zeros(q.shape, jnp.int32)
    for p in range(NP):
        cnt = jnp.where(q % NP == p, counts[p], cnt)
    half = foot_ref.shape[1] // 2
    base = pl.multiple_of((where[1] // 4) * 128, 128)
    turn = 32 * (where[1] % 4)
    first = pltpu.roll(foot_ref[:, pl.ds(base, 128)], (128 - turn) % 128, 1)
    second = pltpu.roll(foot_ref[:, pl.ds(half + base, 128)], (160 - turn) % 128, 1)
    own = jnp.where(lane < 32, first, second)
    first_a_ref[...] = jnp.where((q // NP < cnt) & (lane < 64), own, 0.0)
    traces = traces_ref[:, pl.ds(pl.multiple_of(where[0] * 128, 128), 128)]
    first_c_ref[...] = nn(choose_ref[...], traces, precision=HIGH)


def tree_sum(parts):
    while len(parts) > 1:
        odd = [parts[-1]] if len(parts) % 2 else []
        parts = [a + b for a, b in zip(parts[::2], parts[1::2])] + odd
    return parts[0]


def hals(target, gram, x_ref, new_ref, wide):
    shape = (NP, 128)
    for k in range(KP):
        own = gram(k)
        for t in range(KP):
            entry = jnp.broadcast_to(own[:, t : t + 1], shape)
            wide[KP * k + t] = 1.0 / (entry + RIDGE) if t == k else entry

    def sweep(_, xs):
        xs = list(xs)
        for k in range(KP):
            terms = [wide[KP * k + t] * xs[t] for t in range(KP) if t != k]
            last = terms.pop(k - 1 if k else KP - 2)
            rest = target(k) - tree_sum(terms)
            xs[k] = jnp.maximum((rest - last) * wide[KP * k + k], 0.0)
        return tuple(xs)

    xs = lax.fori_loop(0, SWEEPS, sweep, tuple(x_ref[8 * k : 8 * k + 8, :] for k in range(KP)))
    for k in range(KP):
        new_ref[8 * k : 8 * k + 8, :] = xs[k]


def hals_traces_kernel(counts, got_ref, x_ref, out_ref, new_ref, rows, grams, wide):
    total = tree_sum([got_ref[j] for j in range(got_ref.shape[0])])
    unpack = unpacker(counts)
    gram = total[LIVE:]
    gram = jnp.concatenate([gram[:, :LIVE], gram[:, LIVE:]], axis=0)
    rows[...] = nn(unpack, total[:LIVE], precision=HIGH)
    grams[:, :KP] = nt(unpack, gram, precision=HIGH)
    hals(lambda k: rows[8 * k : 8 * k + 8, :], lambda k: grams[8 * k : 8 * k + 8, :KP], x_ref, new_ref, wide)
    out_ref[...] = nn(packer(counts), new_ref[...], precision=HIGH)


def hals_footprints_kernel(counts, got_ref, x_ref, send_ref, new_ref, rows, grams, wide):
    total = tree_sum([got_ref[j] for j in range(got_ref.shape[0])])
    unpack = unpacker(counts)
    size = total.shape[0] - GRAM
    cols = jnp.concatenate([total[:size, :LIVE], total[:size, LIVE:]], axis=0)
    gram = total[size:]
    gram = jnp.concatenate([gram[:, :LIVE], gram[:, LIVE:]], axis=0)
    rows[:, : 2 * size] = nt(unpack, cols, precision=HIGH)
    rows[:, 2 * size :] = jnp.zeros((KP * NP, 128 - 2 * size), F32)
    grams[:, :KP] = nt(unpack, gram, precision=HIGH)
    hals(lambda k: rows[8 * k : 8 * k + 8, :], lambda k: grams[8 * k : 8 * k + 8, :KP], x_ref, new_ref, wide)
    packed = nn(new_ref[...].T[: 2 * size], unpack, precision=HIGH)
    chunk = jnp.concatenate([packed[:size], packed[size:]], axis=1)
    for j in range(send_ref.shape[0]):
        send_ref[j] = chunk


def footprints_kernel(counts, gathered_ref, out_ref):
    half = gathered_ref.shape[0]
    unpack = unpacker(counts)
    gathered = gathered_ref[...]
    out_ref[:, :half] = nt(unpack, gathered[:, :LIVE], precision=HIGH)
    out_ref[:, half:] = nt(unpack, gathered[:, LIVE:], precision=HIGH)


def traces_kernel(counts, gathered_ref, traces_ref, home_ref, out_ref):
    home = home_ref[...]
    place = nn(home, unpacker(counts), precision=HIGH)
    live = jnp.sum(home, axis=1, keepdims=True) > 0.5
    for h in range(2):
        at = slice(128 * h, 128 * h + 128)
        moved = nn(place, gathered_ref[h], precision=HIGH)
        out_ref[:, at] = jnp.where(live, moved, traces_ref[:, at])


def call(kernel, outs, specs, args, scratch=()):
    return pl.pallas_call(
        kernel,
        out_shape=[jax.ShapeDtypeStruct(s, F32) for s in outs],
        in_specs=specs + [VMEM] * (len(args) - len(specs)),
        out_specs=[VMEM] * len(outs),
        scratch_shapes=list(scratch),
        compiler_params=pltpu.CompilerParams(vmem_limit_bytes=32 * 1024 * 1024),
    )(*args)


def local(sizes, movie, footprints, traces, patch_counts, slot_neuron):
    n_across, n_near, n_far = sizes
    slots, patches, voxels = footprints.shape
    q = slots * patches
    foot = footprints.reshape(q, voxels)
    neuron = slot_neuron.reshape(patches, slots).T.reshape(q)
    live = (jnp.arange(slots, dtype=jnp.int32)[:, None] < patch_counts[None, :]).reshape(q)
    ids = jnp.arange(q, dtype=jnp.int32)
    choose = ((neuron[:, None] == ids[None, :]) & live[:, None]).astype(F32)
    home = ((neuron[None, :] == ids[:, None]) & live[None, :]).astype(F32)
    where = jnp.stack([lax.axis_index("core"), lax.axis_index(NEAR)]).astype(jnp.int32)

    def swap(x, axes):
        return lax.all_to_all(x, axes, 0, 0, tiled=True)

    def cores(x):
        return lax.all_gather(x, "core", axis=0, tiled=False)

    scratch = [pltpu.VMEM((q, 128), F32), pltpu.VMEM((q, 128), F32), pltpu.VMEM((KP * KP, NP, 128), F32)]
    part = voxels // 2 // n_near
    x_c, x_a = call(start_kernel, [(q, 128)] * 2, [SMEM] * 2, [patch_counts, where, foot, traces, choose])
    for step in range(ITERS):
        halves = [(2, LIVE + GRAM, 128)]
        if step == 0:
            buffers = [
                pltpu.VMEM(movie.shape, movie.dtype),
                pltpu.VMEM(foot.shape, F32),
                pltpu.SemaphoreType.DMA((NP + 1,)),
            ]
            specs = [SMEM, HBM, HBM]
            (partial,) = call(first_project_kernel, halves, specs, [patch_counts, foot, movie], buffers)
        else:
            (partial,) = call(project_kernel, halves, [SMEM], [patch_counts, all_a, movie])
        (send,) = call(keep_half_kernel, [(n_across, LIVE + GRAM, 128)], [SMEM], [where, cores(partial)])
        own_c, x_c = call(
            hals_traces_kernel, [(LIVE, 128), (q, 128)], [SMEM], [patch_counts, swap(send, ACROSS), x_c], scratch
        )
        all_c = cores(own_c)
        (send,) = call(correlate_kernel, [(n_near, part + GRAM, 128)], [SMEM], [patch_counts, all_c, movie])
        (send,) = call(keep_part_kernel, [(n_far, part + GRAM, 128)], [], [swap(send, NEAR)])
        send, x_a = call(
            hals_footprints_kernel,
            [(n_near, part, 128), (q, 128)],
            [SMEM],
            [patch_counts, swap(send, FAR), x_a],
            scratch,
        )
        all_a = swap(send, NEAR).reshape(voxels // 2, 128)
    (new_traces,) = call(traces_kernel, [traces.shape], [SMEM], [patch_counts, all_c, traces, home])
    (new_foot,) = call(footprints_kernel, [foot.shape], [SMEM], [patch_counts, all_a])
    return new_foot.reshape(footprints.shape), new_traces


def solution(mesh):
    names = ("x", "zf", "zn", "y", "core", "plane")
    shape = (2, mesh.shape["tm"] // 8, 4, mesh.shape["tile"] // 2, 2, mesh.shape["plane"])
    fine = jax.sharding.Mesh(mesh.devices.reshape(shape), names)
    frames, voxels = names[:3], names[3:]
    sizes = (shape[3] * shape[5], shape[0] * shape[2], shape[1])
    return jax.shard_map(
        functools.partial(local, sizes),
        mesh=fine,
        in_specs=(P(None, voxels, frames), P(None, None, voxels), P(None, frames), P(), P()),
        out_specs=(P(None, None, voxels), P(None, frames)),
        check_vma=False,
    )
```

time: 171 us -> 146 us (0.85)
  blocking collectives: 113 us -> 94.2 us
  waiting for transfers between devices: 19.6 us -> 12.3 us
    all_to_all x6, blocking collectives: 113 us -> 86.7 us  [swap(): return lax.all_to_all(x, axes, 0, 0, tiled=True)]
    all_gather x0 -> x4, blocking collectives: none -> 7.51 us  [cores(): return lax.all_gather(x, 'core', axis=0, tiled=False)]
    all_to_all x2, waiting for transfers between devices: 19.6 us -> 12.3 us  [swap(): return lax.all_to_all(x, axes, 0, 0, tiled=True)]
    pallas_call x11 -> x15, Pallas kernels: 20.4 us -> 21.8 us  [call(): pl.pallas_call(kernel, out_shape=[jax.ShapeDtypeStruct(s, F32) for s in o...]
where the time goes in v2:
time: 146 us; the launch traced here: 145 us
  blocking collectives  94.2 us (65%)
  Pallas kernels  21.8 us (15%)
  starting transfers between devices  12.5 us (9%)
  waiting for transfers between devices  12.3 us (8%)
  local copies, waits for them, and re-layouts  3.55 us (2%)
    all_to_all x6, blocking collectives, swap(): return lax.all_to_all(x, axes, 0, 0, tiled=True)  86.7 us
    pallas_call x15, Pallas kernels, call(): pl.pallas_call(kernel, out_shape=[jax.ShapeDtypeStruct(s, F32) for s in o...  21.8 us
    all_to_all x2, starting transfers between devices, swap(): return lax.all_to_all(x, axes, 0, 0, tiled=True)  12.5 us
    all_to_all x2, waiting for transfers between devices, swap(): return lax.all_to_all(x, axes, 0, 0, tiled=True)  12.3 us
    all_gather x4, blocking collectives, cores(): return lax.all_gather(x, 'core', axis=0, tiled=False)  7.51 us
    unnamed x16, local copies, waits for them, and re-layouts  3.21 us
  transfers between devices with their start and end apart: 2, of which 2 were waited for; matrix products, arithmetic and copies ran while one was open for 0% of the time, Pallas kernels for 2%

profile of v2, /device:TPU:8, one launch (start us, length us, event | category | flops | bytes accessed | tf_op | source)
XLA Modules:
  0.0 145.4 jit_solution(1481295630706036562)
XLA Ops:
  0.7 1.6 %copy-done = bf16[8,512,256]{2,1,0:T(8,128)(2,1)S(1)} copy-done((bf16[8,512,256]{2,1,0:T(8,128)(2,1)S(1)}, bf16[8,512,256]{2,1,0:T(8,128)(2,1)}, u32[]{:S(2)}) %copy-start) | copy-done | bytes 2097176
  3.9 2.4 %shard_map.68 = f32[2,72,128]{2,1,0:T(8,128)S(1)} custom-call(s32[8]{0:T(128)S(1)} %copy-done.5, f32[128,512]{1,0:T(8,128)S(1)} %bitcast.11, bf16[8,512,256]{2,1,0:T(8,128)(2,1)S(1)} %copy-done), custom_call_target="tpu_custom_call" | custom-call | tf_op jit(solution)/shard_map/pallas_call | solution.py:250
  6.3 1.9 %all-gather = f32[4,72,128]{2,1,0:T(8,128)S(1)} all-gather(f32[2,72,128]{2,1,0:T(8,128)S(1)} %shard_map.68), channel_id=2, replica_groups=mesh['x'=2,'zf'=4,'zn'=4,'y'=4,'core'=2,'plane'=2] {'core'}, dimensions={0}, use_global_device_ids=true | all-gather | bytes 221184 | tf_op jit(solution)/shard_map/all_gather | solution.py:276
  9.6 9.2 %all-to-all-start = ((f32[8,72,128]{2,1,0:T(8,128)}), f32[8,72,128]{2,1,0:T(8,128)S(1)}, u32[]{:S(2)}, u32[]{:S(2)}) async-start(f32[8,72,128]{2,1,0:T(8,128)} %shard_map.69), calls=%async_computation | async-start | bytes 589824 | tf_op jit(solution)/shard_map/all_to_all | solution.py:273
  20.0 6.6 %all-to-all-done.got_ref = f32[8,72,128]{2,1,0:T(8,128)S(1)} async-done(((f32[8,72,128]{2,1,0:T(8,128)}), f32[8,72,128]{2,1,0:T(8,128)S(1)}, u32[]{:S(2)}, u32[]{:S(2)}) %all-to-all-start) | async-done | bytes 294944 | tf_op jit(solution)/shard_map/all_to_all | solution.py:273
  26.6 1.8 %shard_map.71 = (f32[64,128]{1,0:T(8,128)S(1)}, f32[128,128]{1,0:T(8,128)S(1)}) custom-call(s32[8]{0:T(128)S(1)} %copy-done.6, f32[8,72,128]{2,1,0:T(8,128)S(1)} %all-to-all-done.got_ref, f32[128,128]{1,0:T(8,128)S(1)} %get-tuple-element.10.x_ref), custom_call_target="tpu_custom_call" | custom-call | tf_op jit(solution)/shard_map/pallas_call | solution.py:250
  28.5 1.9 %all-gather.1 = f32[128,128]{1,0:T(8,128)S(1)} all-gather(f32[64,128]{1,0:T(8,128)S(1)} %get-tuple-element.11), channel_id=3, replica_groups=mesh['x'=2,'zf'=4,'zn'=4,'y'=4,'core'=2,'plane'=2] {'core'}, dimensions={0}, use_global_device_ids=true | all-gather | bytes 98304 | tf_op jit(solution)/shard_map/all_gather | solution.py:276
  30.4 1.6 %shard_map.72 = f32[8,40,128]{2,1,0:T(8,128)S(1)} custom-call(s32[8]{0:T(128)S(1)} %copy-done.6, f32[2,64,128]{2,1,0:T(8,128)S(1)} %bitcast.19, bf16[8,512,256]{2,1,0:T(8,128)(2,1)S(1)} %copy-done.1), custom_call_target="tpu_custom_call" | custom-call | tf_op jit(solution)/shard_map/pallas_call | solution.py:250
  32.0 11.9 %all_to_all.40.got_ref = f32[8,40,128]{2,1,0:T(8,128)S(1)} all-to-all(f32[8,40,128]{2,1,0:T(8,128)S(1)} %shard_map.72), channel_id=1, replica_groups=mesh['x'=2,'zf'=4,'zn'=4,'y'=4,'core'=2,'plane'=2] {'x','zn'}, dimensions={0} | all-to-all | bytes 327680 | tf_op jit(solution)/shard_map/all_to_all | solution.py:273
  43.9 25.3 %all_to_all.41.got_ref = f32[4,40,128]{2,1,0:T(8,128)S(1)} all-to-all(f32[4,40,128]{2,1,0:T(8,128)S(1)} %shard_map.73), channel_id=1, replica_groups=mesh['x'=2,'zf'=4,'zn'=4,'y'=4,'core'=2,'plane'=2] {'zf'}, dimensions={0} | all-to-all | bytes 163840 | tf_op jit(solution)/shard_map/all_to_all | solution.py:273
  69.3 2.0 %shard_map.74 = (f32[8,32,128]{2,1,0:T(8,128)S(1)}, f32[128,128]{1,0:T(8,128)S(1)}) custom-call(s32[8]{0:T(128)S(1)} %copy-done.6, f32[4,40,128]{2,1,0:T(8,128)S(1)} %all_to_all.41.got_ref, f32[128,128]{1,0:T(8,128)S(1)} %get-tuple-element.12.x_ref), custom_call_target="tpu_custom_call" | custom-call | tf_op jit(solution)/shard_map/pallas_call | solution.py:250
  71.2 10.1 %all_to_all.42 = f32[8,32,128]{2,1,0:T(8,128)S(1)} all-to-all(f32[8,32,128]{2,1,0:T(8,128)S(1)} %get-tuple-element.13), channel_id=1, replica_groups=mesh['x'=2,'zf'=4,'zn'=4,'y'=4,'core'=2,'plane'=2] {'x','zn'}, dimensions={0} | all-to-all | bytes 262144 | tf_op jit(solution)/shard_map/all_to_all | solution.py:273
  82.7 1.9 %all-gather.2 = f32[4,72,128]{2,1,0:T(8,128)S(1)} all-gather(f32[2,72,128]{2,1,0:T(8,128)S(1)} %shard_map.75), channel_id=4, replica_groups=mesh['x'=2,'zf'=4,'zn'=4,'y'=4,'core'=2,'plane'=2] {'core'}, dimensions={0}, use_global_device_ids=true | all-gather | bytes 221184 | tf_op jit(solution)/shard_map/all_gather | solution.py:276
  85.2 13.1 %all_to_all.43.got_ref = f32[8,72,128]{2,1,0:T(8,128)S(1)} all-to-all(f32[8,72,128]{2,1,0:T(8,128)S(1)} %shard_map.76), channel_id=1, replica_groups=mesh['x'=2,'zf'=4,'zn'=4,'y'=4,'core'=2,'plane'=2] {'y','plane'}, dimensions={0} | all-to-all | bytes 589824 | tf_op jit(solution)/shard_map/all_to_all | solution.py:273
  98.3 2.3 %shard_map.77 = (f32[64,128]{1,0:T(8,128)S(1)}, f32[128,128]{1,0:T(8,128)}) custom-call(s32[8]{0:T(128)S(1)} %copy-done.6, f32[8,72,128]{2,1,0:T(8,128)S(1)} %all_to_all.43.got_ref, f32[128,128]{1,0:T(8,128)S(1)} %get-tuple-element.14.x_ref), custom_call_target="tpu_custom_call" | custom-call | tf_op jit(solution)/shard_map/pallas_call | solution.py:250
  100.6 1.8 %all-gather.3 = f32[128,128]{1,0:T(8,128)S(1)} all-gather(f32[64,128]{1,0:T(8,128)S(1)} %get-tuple-element.15), channel_id=5, replica_groups=mesh['x'=2,'zf'=4,'zn'=4,'y'=4,'core'=2,'plane'=2] {'core'}, dimensions={0}, use_global_device_ids=true | all-gather | bytes 98304 | tf_op jit(solution)/shard_map/all_gather | solution.py:276
  102.4 1.6 %shard_map.78 = f32[8,40,128]{2,1,0:T(8,128)S(1)} custom-call(s32[8]{0:T(128)S(1)} %copy-done.6, f32[2,64,128]{2,1,0:T(8,128)S(1)} %bitcast.13, bf16[8,512,256]{2,1,0:T(8,128)(2,1)S(1)} %copy-done.1), custom_call_target="tpu_custom_call" | custom-call | tf_op jit(solution)/shard_map/pallas_call | solution.py:250
  104.0 10.7 %all_to_all.44.got_ref = f32[8,40,128]{2,1,0:T(8,128)S(1)} all-to-all(f32[8,40,128]{2,1,0:T(8,128)S(1)} %shard_map.78), channel_id=1, replica_groups=mesh['x'=2,'zf'=4,'zn'=4,'y'=4,'core'=2,'plane'=2] {'x','zn'}, dimensions={0} | all-to-all | bytes 327680 | tf_op jit(solution)/shard_map/all_to_all | solution.py:273
  114.7 15.5 %all_to_all.45.got_ref = f32[4,40,128]{2,1,0:T(8,128)S(1)} all-to-all(f32[4,40,128]{2,1,0:T(8,128)S(1)} %shard_map.79), channel_id=1, replica_groups=mesh['x'=2,'zf'=4,'zn'=4,'y'=4,'core'=2,'plane'=2] {'zf'}, dimensions={0} | all-to-all | bytes 163840 | tf_op jit(solution)/shard_map/all_to_all | solution.py:273
  130.2 2.6 %shard_map.80 = (f32[8,32,128]{2,1,0:T(8,128)}, f32[128,128]{1,0:T(8,128)}) custom-call(s32[8]{0:T(128)S(1)} %copy-done.6, f32[4,40,128]{2,1,0:T(8,128)S(1)} %all_to_all.45.got_ref, f32[128,128]{1,0:T(8,128)S(1)} %get-tuple-element.16.x_ref), custom_call_target="tpu_custom_call" | custom-call | tf_op jit(solution)/shard_map/pallas_call | solution.py:250
  132.9 3.4 %all-to-all-start.7 = ((f32[8,32,128]{2,1,0:T(8,128)}), f32[8,32,128]{2,1,0:T(8,128)S(1)}, u32[]{:S(2)}, u32[]{:S(2)}) async-start(f32[8,32,128]{2,1,0:T(8,128)} %get-tuple-element.17), calls=%async_computation.7 | async-start | bytes 262144 | tf_op jit(solution)/shard_map/all_to_all | solution.py:273
  136.3 1.8 %shard_map.82 = f32[128,256]{1,0:T(8,128)} custom-call(s32[8]{0:T(128)S(1)} %copy-done.6, f32[2,64,128]{2,1,0:T(8,128)S(1)} %bitcast.14, f32[128,256]{1,0:T(8,128)S(1)} %copy-done.4, f32[128,128]{1,0:T(8,128)S(1)} %get-tuple-element.18.home_ref), custom_call_target="tpu_custom_call" | custom-call | tf_op jit(solution)/shard_map/pallas_call | solution.py:250
  138.0 5.7 %all-to-all-done.7 = f32[8,32,128]{2,1,0:T(8,128)S(1)} async-done(((f32[8,32,128]{2,1,0:T(8,128)}), f32[8,32,128]{2,1,0:T(8,128)S(1)}, u32[]{:S(2)}, u32[]{:S(2)}) %all-to-all-start.7) | async-done | bytes 131104 | tf_op jit(solution)/shard_map/all_to_all | solution.py:273
  143.7 1.7 %shard_map.81 = f32[128,512]{1,0:T(8,128)} custom-call(s32[8]{0:T(128)S(1)} %copy-done.6, f32[256,128]{1,0:T(8,128)S(1)} %bitcast.18), custom_call_target="tpu_custom_call" | custom-call | tf_op jit(solution)/shard_map/pallas_call | solution.py:250
  (28 shorter events, 6.1 us)
Async XLA Ops:
  0.6 18.1 %copy-start.6 = (s32[8]{0:T(128)S(1)}, s32[8]{0:T(128)}, u32[]{:S(2)}) copy-start(s32[8]{0:T(128)} %counts.21) | copy-start | bytes 100
  0.6 18.1 %copy-start.7 = (s32[128]{0:T(128)S(1)}, s32[128]{0:T(128)}, u32[]{:S(2)}) copy-start(s32[128]{0:T(128)} %param.9) | copy-start | bytes 1540
  0.7 1.6 %copy-start = (bf16[8,512,256]{2,1,0:T(8,128)(2,1)S(1)}, bf16[8,512,256]{2,1,0:T(8,128)(2,1)}, u32[]{:S(2)}) copy-start(bf16[8,512,256]{2,1,0:T(8,128)(2,1)} %movie_ref.7) | copy-start | bytes 6291460
  2.3 0.9 copy-start.2
  3.2 0.7 copy-start.5
  3.9 15.3 %copy-start.3 = (f32[16,8,512]{2,1,0:T(8,128)S(1)}, f32[16,8,512]{2,1,0:T(8,128)}, u32[]{:S(2)}) copy-start(f32[16,8,512]{2,1,0:T(8,128)} %param.6) | copy-start | bytes 786436
  3.9 15.3 %copy-start.4 = (f32[128,256]{1,0:T(8,128)S(1)}, f32[128,256]{1,0:T(8,128)}, u32[]{:S(2)}) copy-start(f32[128,256]{1,0:T(8,128)} %traces_ref.3) | copy-start | bytes 393220
  3.9 26.5 %copy-start.1 = (bf16[8,512,256]{2,1,0:T(8,128)(2,1)S(1)}, bf16[8,512,256]{2,1,0:T(8,128)(2,1)}, u32[]{:S(2)}) copy-start(bf16[8,512,256]{2,1,0:T(8,128)(2,1)} %movie_ref.7) | copy-start | bytes 6291460
  9.6 17.0 %all-to-all-start = ((f32[8,72,128]{2,1,0:T(8,128)}), f32[8,72,128]{2,1,0:T(8,128)S(1)}, u32[]{:S(2)}, u32[]{:S(2)}) async-start(f32[8,72,128]{2,1,0:T(8,128)} %shard_map.69), calls=%async_computation | async-start | bytes 589824 | tf_op jit(solution)/shard_map/all_to_all | solution.py:273
  132.9 10.8 %all-to-all-start.7 = ((f32[8,32,128]{2,1,0:T(8,128)}), f32[8,32,128]{2,1,0:T(8,128)S(1)}, u32[]{:S(2)}, u32[]{:S(2)}) async-start(f32[8,32,128]{2,1,0:T(8,128)} %get-tuple-element.17), calls=%async_computation.7 | async-start | bytes 262144 | tf_op jit(solution)/shard_map/all_to_all | solution.py:273

commit v3 on v2

v3 whole, which is shorter than its diff:
```python
import functools

import jax
import jax.numpy as jnp
from jax import lax
from jax.experimental import pallas as pl
from jax.experimental.pallas import tpu as pltpu
from jax.sharding import PartitionSpec as P

ITERS = 2
SWEEPS = 3
RIDGE = 1.0
HIGH = lax.Precision.HIGHEST
F32 = jnp.float32
BF16 = jnp.bfloat16
KP = 16
NP = 8
LIVE = 64
ACROSS = ("y", "plane")
NEAR = ("x", "zn")
FAR = "zf"
GRAM = 8

VMEM = pl.BlockSpec(memory_space=pltpu.VMEM)
HBM = pl.BlockSpec(memory_space=pltpu.HBM)


def nn(a, b, **kw):
    return lax.dot_general(a, b, (((1,), (0,)), ((), ())), preferred_element_type=F32, **kw)


def nt(a, b, **kw):
    return lax.dot_general(a, b, (((1,), (1,)), ((), ())), preferred_element_type=F32, **kw)


def split(x):
    high = x.astype(BF16)
    rest = x - high.astype(F32)
    middle = rest.astype(BF16)
    return [high, middle, (rest - middle.astype(F32)).astype(BF16)]


def choose_rows(pick, x):
    return nn(jnp.concatenate([pick.astype(BF16)] * 3, axis=1), jnp.concatenate(split(x), axis=0))


def choose_cols(pick, x):
    return nt(jnp.concatenate([pick.astype(BF16)] * 3, axis=1), jnp.concatenate(split(x), axis=1))


def spread(counts_ref):
    return [jnp.broadcast_to(counts_ref[:, p : p + 1], (1, 128)) for p in range(NP)]


def fit(row, shape):
    return row[:, : shape[1]] if shape[1] <= 128 else jnp.concatenate([row] * (shape[1] // 128), axis=1)


def offsets(counts, shape):
    offs = [jnp.zeros((1, 128), jnp.int32)]
    for p in range(NP - 1):
        offs.append(offs[-1] + counts[p])
    return [fit(off, shape) for off in offs]


def iota(shape, dim):
    return lax.broadcasted_iota(jnp.int32, shape, dim)


def patch_and_slot(counts, shape, dim):
    offs = offsets(counts, shape)
    r = iota(shape, dim)
    patch = jnp.zeros(shape, jnp.int32)
    slot = r
    for p in range(1, NP):
        at = r >= offs[p]
        patch = jnp.where(at, p, patch)
        slot = jnp.where(at, r - offs[p], slot)
    return patch, slot


def unpacker(counts):
    shape = (NP, LIVE)
    offs = offsets(counts, shape)
    p, r = iota(shape, 0), iota(shape, 1)
    off = jnp.zeros(shape, jnp.int32)
    cnt = jnp.zeros(shape, jnp.int32)
    for i in range(NP):
        off = jnp.where(p == i, offs[i], off)
        cnt = jnp.where(p == i, fit(counts[i], shape), cnt)
    return jnp.concatenate([((r == off + s) & (s < cnt)).astype(F32) for s in range(KP)], axis=0)


def packer(counts):
    shape = (LIVE, KP * NP)
    patch, slot = patch_and_slot(counts, shape, 0)
    return (iota(shape, 1) == slot * NP + patch).astype(F32)


def gram_chunk(counts, full):
    shape = (LIVE, LIVE)
    patch_a, _ = patch_and_slot(counts, shape, 0)
    patch_b, _ = patch_and_slot(counts, shape, 1)
    own = jnp.where(patch_a == patch_b, full, 0.0)
    _, slot = patch_and_slot(counts, (KP, LIVE), 1)
    pick = (slot == iota((KP, LIVE), 0)).astype(F32)
    by_slot = choose_rows(pick, own)
    return jnp.concatenate([by_slot[:8], by_slot[8:]], axis=1)


def project_packed(counts, packed, movie, out_ref):
    low = packed.astype(BF16)
    patch, _ = patch_and_slot(counts, low.shape, 0)
    zero = jnp.zeros_like(low)
    total = None
    for p in range(NP):
        term = nn(jnp.where(patch == p, low, zero), movie(p))
        total = term if p == 0 else total + term
    gram = gram_chunk(counts, nt(packed, packed, precision=HIGH))
    for h in range(2):
        out_ref[h, :LIVE, :] = total[:, 128 * h : 128 * h + 128]
        out_ref[h, LIVE:, :] = gram


def neuron_slots(neuron):
    shape = (KP * NP, KP * NP)
    return (iota(shape, 0) == neuron).astype(BF16)


def first_columns(counts, neuron, foot_ref, traces, first_c_ref, first_a_ref):
    shape = (KP * NP, KP * NP)
    q, lane = iota(shape, 0), iota(shape, 1)
    cnt = jnp.zeros(shape, jnp.int32)
    for p in range(NP):
        cnt = jnp.where(q % NP == p, counts[p], cnt)
    live = q // NP < cnt
    half = foot_ref.shape[1] // 2
    near = lax.axis_index(NEAR)
    base = pl.multiple_of((near // 4) * 128, 128)
    turn = 32 * (near % 4)
    first = pltpu.roll(foot_ref[:, pl.ds(base, 128)], (128 - turn) % 128, 1)
    second = pltpu.roll(foot_ref[:, pl.ds(half + base, 128)], (160 - turn) % 128, 1)
    own = jnp.where(lane < 32, first, second)
    first_a_ref[...] = jnp.where(live & (lane < 64), own, 0.0)
    order = (lane == (q % NP) * KP + q // NP).astype(BF16)
    choose = nt(order, neuron_slots(neuron))
    first_c_ref[...] = jnp.where(live, choose_rows(choose, traces), 0.0)


def first_kernel(counts_hbm, neuron_hbm, foot_hbm, traces_hbm, movie_hbm, *refs):
    out_ref, first_c_ref, first_a_ref, counts_ref, neuron_ref, foot_ref, traces_ref, movie_ref, sems = refs
    half = traces_ref.shape[1]
    own = pl.ds(pl.multiple_of(lax.axis_index("core") * half, half), half)
    pairs = [
        (counts_hbm, counts_ref),
        (neuron_hbm, neuron_ref),
        (foot_hbm, foot_ref),
        (traces_hbm.at[:, own], traces_ref),
    ]
    pairs += [(movie_hbm.at[p], movie_ref.at[p]) for p in range(NP)]
    copies = [pltpu.make_async_copy(src, dst, sems.at[i]) for i, (src, dst) in enumerate(pairs)]
    for copy in copies:
        copy.start()
    for copy in copies[:4]:
        copy.wait()
    counts = spread(counts_ref)
    packed = choose_rows(packer(counts), foot_ref[...])

    def movie(p):
        copies[4 + p].wait()
        return movie_ref[p]

    project_packed(counts, packed, movie, out_ref)
    first_columns(counts, neuron_ref[...], foot_ref, traces_ref[...], first_c_ref, first_a_ref)


def project_kernel(counts_ref, gathered_ref, movie_ref, out_ref):
    counts = spread(counts_ref)
    rows = jnp.concatenate([gathered_ref[:128].T, gathered_ref[128:].T], axis=1)
    packed = jnp.concatenate([rows[:LIVE], rows[LIVE:]], axis=1)
    project_packed(counts, packed, lambda p: movie_ref[p], out_ref)


def keep_half_kernel(got_ref, send_ref):
    core = lax.axis_index("core")
    kept = got_ref[0, core] + got_ref[1, core]
    for j in range(send_ref.shape[0]):
        send_ref[j] = kept


def keep_part_kernel(got_ref, send_ref):
    total = tree_sum([got_ref[j] for j in range(got_ref.shape[0])])
    for j in range(send_ref.shape[0]):
        send_ref[j] = total


def correlate_kernel(counts_ref, gathered_ref, movie_ref, send_ref):
    counts = spread(counts_ref)
    rows = jnp.concatenate([gathered_ref[0], gathered_ref[1]], axis=1)
    gram = gram_chunk(counts, nt(rows, rows, precision=HIGH))
    low = rows.T.astype(BF16)
    patch, _ = patch_and_slot(counts, low.shape, 1)
    zero = jnp.zeros_like(low)
    total = None
    for p in range(NP):
        term = nn(movie_ref[p], jnp.where(patch == p, low, zero))
        total = term if p == 0 else total + term
    half = total.shape[0] // 2
    chunks = jnp.concatenate([total[:half], total[half:]], axis=1)
    n = send_ref.shape[0]
    size = half // n
    for i in range(n):
        send_ref[i, :size, :] = chunks[size * i : size * i + size]
        send_ref[i, size:, :] = gram


def tree_sum(parts):
    while len(parts) > 1:
        odd = [parts[-1]] if len(parts) % 2 else []
        parts = [a + b for a, b in zip(parts[::2], parts[1::2])] + odd
    return parts[0]


def hals(target, gram, x_ref, new_ref, wide):
    shape = (NP, 128)
    for k in range(KP):
        own = gram(k)
        scale = 1.0 / (jnp.broadcast_to(own[:, k : k + 1], shape) + RIDGE)
        for t in range(KP):
            entry = jnp.broadcast_to(own[:, t : t + 1], shape)
            wide[KP * k + t] = entry * scale
        wide[KP * k + k] = target(k) * scale

    def sweep(_, xs):
        xs = list(xs)
        for k in range(KP):
            terms = [wide[KP * k + t] * xs[t] for t in range(KP) if t != k]
            last = terms.pop(k - 1 if k else KP - 2)
            rest = wide[KP * k + k] - tree_sum(terms)
            xs[k] = jnp.maximum(rest - last, 0.0)
        return tuple(xs)

    xs = tuple(x_ref[8 * k : 8 * k + 8, :] for k in range(KP))
    for sweep_index in range(SWEEPS):
        xs = sweep(sweep_index, xs)
    for k in range(KP):
        new_ref[8 * k : 8 * k + 8, :] = xs[k]


def hals_traces_kernel(counts_ref, got_ref, x_ref, out_ref, new_ref, rows, grams, wide):
    counts = spread(counts_ref)
    total = tree_sum([got_ref[j] for j in range(got_ref.shape[0])])
    unpack = unpacker(counts)
    gram = total[LIVE:]
    gram = jnp.concatenate([gram[:, :LIVE], gram[:, LIVE:]], axis=0)
    rows[...] = choose_rows(unpack, total[:LIVE])
    grams[:, :KP] = choose_cols(unpack, gram)
    hals(lambda k: rows[8 * k : 8 * k + 8, :], lambda k: grams[8 * k : 8 * k + 8, :KP], x_ref, new_ref, wide)
    out_ref[...] = choose_rows(packer(counts), new_ref[...])


def hals_footprints_kernel(counts_ref, got_ref, x_ref, send_ref, new_ref, rows, grams, wide):
    counts = spread(counts_ref)
    total = tree_sum([got_ref[j] for j in range(got_ref.shape[0])])
    unpack = unpacker(counts)
    size = total.shape[0] - GRAM
    cols = jnp.concatenate([total[:size, :LIVE], total[:size, LIVE:]], axis=0)
    gram = total[size:]
    gram = jnp.concatenate([gram[:, :LIVE], gram[:, LIVE:]], axis=0)
    rows[:, : 2 * size] = choose_cols(unpack, cols)
    rows[:, 2 * size :] = jnp.zeros((KP * NP, 128 - 2 * size), F32)
    grams[:, :KP] = choose_cols(unpack, gram)
    hals(lambda k: rows[8 * k : 8 * k + 8, :], lambda k: grams[8 * k : 8 * k + 8, :KP], x_ref, new_ref, wide)
    packed = choose_rows(packer(counts), new_ref[...]).T
    chunk = jnp.concatenate([packed[:size], packed[size : 2 * size]], axis=1)
    for j in range(send_ref.shape[0]):
        send_ref[j] = chunk


def last_kernel(counts_ref, neuron_ref, all_a_ref, all_c_ref, traces_ref, foot_ref, out_ref):
    counts = spread(counts_ref)
    shape = (LIVE, KP * NP)
    patch, slot = patch_and_slot(counts, shape, 0)
    kept = (iota(shape, 1) == patch * KP + slot).astype(BF16)
    place = nt(neuron_slots(neuron_ref[...]), kept)
    live = jnp.sum(place, axis=1, keepdims=True) > 0.5
    for h in range(2):
        at = slice(128 * h, 128 * h + 128)
        out_ref[:, at] = jnp.where(live, choose_rows(place, all_c_ref[h]), traces_ref[:, at])
    half = all_a_ref.shape[0]
    unpack = unpacker(counts)
    all_a = all_a_ref[...]
    foot_ref[:, :half] = choose_cols(unpack, all_a[:, :LIVE])
    foot_ref[:, half:] = choose_cols(unpack, all_a[:, LIVE:])


def call(kernel, outs, specs, args, scratch=(), grant=32):
    return pl.pallas_call(
        kernel,
        out_shape=[jax.ShapeDtypeStruct(s, F32) for s in outs],
        in_specs=specs + [VMEM] * (len(args) - len(specs)),
        out_specs=[VMEM] * len(outs),
        scratch_shapes=list(scratch),
        compiler_params=pltpu.CompilerParams(vmem_limit_bytes=int(grant * 1024 * 1024)),
    )(*args)


def local(sizes, movie, footprints, traces, patch_counts, slot_neuron):
    n_across, n_near, n_far = sizes
    slots, patches, voxels = footprints.shape
    q = slots * patches
    foot = footprints.reshape(q, voxels)
    counts = patch_counts.reshape(1, patches)
    neuron = slot_neuron.reshape(1, q)

    def swap(x, axes):
        return lax.all_to_all(x, axes, 0, 0, tiled=True)

    def cores(x):
        return lax.all_gather(x, "core", axis=0, tiled=False)

    square = pltpu.VMEM((q, 128), F32)
    state = [(q, 128)]
    part = voxels // 2 // n_near
    for step in range(ITERS):
        halves = [(2, LIVE + GRAM, 128)]
        scratch = [square, square, pltpu.VMEM((KP * KP, NP, 128), F32)]
        if step == ITERS - 1:
            state, scratch = [], [square] + scratch
        if step == 0:
            loaded = [counts, neuron, foot, traces, movie]
            shapes = [counts.shape, neuron.shape, foot.shape, (q, traces.shape[1] // 2), movie.shape]
            buffers = [pltpu.VMEM(shape, x.dtype) for shape, x in zip(shapes, loaded)]
            buffers.append(pltpu.SemaphoreType.DMA((4 + patches,)))
            outs = halves + [(q, 128)] * 2
            partial, first_c, first_a = call(first_kernel, outs, [HBM] * 5, loaded, buffers, 53.5)
            x_c, x_a = [first_c], [first_a]
        else:
            (partial,) = call(project_kernel, halves, [], [counts, all_a, movie])
        (send,) = call(keep_half_kernel, [(n_across, LIVE + GRAM, 128)], [], [cores(partial)])
        own_c, *x_c = call(
            hals_traces_kernel, [(LIVE, 128)] + state, [], [counts, swap(send, ACROSS), *x_c], scratch
        )
        all_c = cores(own_c)
        (send,) = call(correlate_kernel, [(n_near, part + GRAM, 128)], [], [counts, all_c, movie])
        (send,) = call(keep_part_kernel, [(n_far, part + GRAM, 128)], [], [swap(send, NEAR)])
        send, *x_a = call(
            hals_footprints_kernel,
            [(n_near, part, 128)] + state,
            [],
            [counts, swap(send, FAR), *x_a],
            scratch,
        )
        all_a = swap(send, NEAR).reshape(voxels // 2, 128)
    last = [counts, neuron, all_a, all_c, traces]
    new_foot, new_traces = call(last_kernel, [foot.shape, traces.shape], [], last)
    return new_foot.reshape(footprints.shape), new_traces


def solution(mesh):
    names = ("x", "zf", "zn", "y", "core", "plane")
    shape = (2, mesh.shape["tm"] // 8, 4, mesh.shape["tile"] // 2, 2, mesh.shape["plane"])
    fine = jax.sharding.Mesh(mesh.devices.reshape(shape), names)
    frames, voxels = names[:3], names[3:]
    sizes = (shape[3] * shape[5], shape[0] * shape[2], shape[1])
    return jax.shard_map(
        functools.partial(local, sizes),
        mesh=fine,
        in_specs=(P(None, voxels, frames), P(None, None, voxels), P(None, frames), P(), P()),
        out_specs=(P(None, None, voxels), P(None, frames)),
        check_vma=False,
    )
```

time: 146 us -> 137 us (0.938)
  the two profiles are of different devices: /device:TPU:8 before, /device:TPU:2 now
where the time goes in v3:
time: 137 us; the launch traced here: 136 us
  blocking collectives  122 us (89%)
  Pallas kernels  11.6 us (8%)
  local copies, waits for them, and re-layouts  2.21 us (2%)
    all_to_all x8, blocking collectives, swap(): return lax.all_to_all(x, axes, 0, 0, tiled=True)  114 us
    pallas_call x13, Pallas kernels, call(): pl.pallas_call(kernel, out_shape=[jax.ShapeDtypeStruct(s, F32) for s in o...  11.6 us
    all_gather x4, blocking collectives, cores(): return lax.all_gather(x, 'core', axis=0, tiled=False)  7.6 us

profile of v3, /device:TPU:2, one launch (start us, length us, event | category | flops | bytes accessed | tf_op | source)
XLA Modules:
  0.0 136.2 jit_solution(1297827782938921881)
XLA Ops:
  0.6 0.9 copy-done.1
  1.5 0.7 copy-done.2
  2.2 0.7 copy-done.3
  2.9 2.9 %shard_map.68 = (f32[2,72,128]{2,1,0:T(8,128)S(1)}, f32[128,128]{1,0:T(8,128)S(1)}, f32[128,128]{1,0:T(8,128)S(1)}) custom-call(s32[1,8]{1,0:T(1,128)S(1)} %bitcast.17, s32[1,128]{1,0:T(1,128)S(1)} %bitcast.26, f32[128,512]{1,0:T(8,128)} %bitcast.28, f32[128,256]{1,0:T(8,128)S(1)} %copy-done.1, bf16[8,512,256]{2,1,0:T(8,128)(2,1)} %movie_ref.5), custom_call_target="tpu_custom_call" | custom-call | tf_op jit(solution)/shard_map/pallas_call | solution.py:298
  5.7 1.9 %all-gather = f32[4,72,128]{2,1,0:T(8,128)S(1)} all-gather(f32[2,72,128]{2,1,0:T(8,128)S(1)} %get-tuple-element.11), channel_id=2, replica_groups=mesh['x'=2,'zf'=4,'zn'=4,'y'=4,'core'=2,'plane'=2] {'core'}, dimensions={0}, use_global_device_ids=true | all-gather | bytes 221184 | tf_op jit(solution)/shard_map/all_gather | solution.py:320
  7.7 15.5 %all_to_all.40.got_ref = f32[8,72,128]{2,1,0:T(8,128)S(1)} all-to-all(f32[8,72,128]{2,1,0:T(8,128)S(1)} %shard_map.69), channel_id=1, replica_groups=mesh['x'=2,'zf'=4,'zn'=4,'y'=4,'core'=2,'plane'=2] {'y','plane'}, dimensions={0} | all-to-all | bytes 589824 | tf_op jit(solution)/shard_map/all_to_all | solution.py:317
  23.1 1.1 shard_map.70
  24.2 1.9 %all-gather.1 = f32[128,128]{1,0:T(8,128)S(1)} all-gather(f32[64,128]{1,0:T(8,128)S(1)} %get-tuple-element.13), channel_id=3, replica_groups=mesh['x'=2,'zf'=4,'zn'=4,'y'=4,'core'=2,'plane'=2] {'core'}, dimensions={0}, use_global_device_ids=true | all-gather | bytes 98304 | tf_op jit(solution)/shard_map/all_gather | solution.py:320
  26.1 1.0 shard_map.71
  27.2 13.9 %all_to_all.41.got_ref = f32[8,40,128]{2,1,0:T(8,128)S(1)} all-to-all(f32[8,40,128]{2,1,0:T(8,128)S(1)} %shard_map.71), channel_id=1, replica_groups=mesh['x'=2,'zf'=4,'zn'=4,'y'=4,'core'=2,'plane'=2] {'x','zn'}, dimensions={0} | all-to-all | bytes 327680 | tf_op jit(solution)/shard_map/all_to_all | solution.py:317
  41.1 25.3 %all_to_all.42.got_ref = f32[4,40,128]{2,1,0:T(8,128)S(1)} all-to-all(f32[4,40,128]{2,1,0:T(8,128)S(1)} %shard_map.72), channel_id=1, replica_groups=mesh['x'=2,'zf'=4,'zn'=4,'y'=4,'core'=2,'plane'=2] {'zf'}, dimensions={0} | all-to-all | bytes 163840 | tf_op jit(solution)/shard_map/all_to_all | solution.py:317
  66.4 1.2 shard_map.73
  67.6 10.1 %all_to_all.43 = f32[8,32,128]{2,1,0:T(8,128)S(1)} all-to-all(f32[8,32,128]{2,1,0:T(8,128)S(1)} %get-tuple-element.15), channel_id=1, replica_groups=mesh['x'=2,'zf'=4,'zn'=4,'y'=4,'core'=2,'plane'=2] {'x','zn'}, dimensions={0} | all-to-all | bytes 262144 | tf_op jit(solution)/shard_map/all_to_all | solution.py:317
  77.7 0.7 shard_map.74
  78.5 2.0 %all-gather.2 = f32[4,72,128]{2,1,0:T(8,128)S(1)} all-gather(f32[2,72,128]{2,1,0:T(8,128)S(1)} %shard_map.74), channel_id=4, replica_groups=mesh['x'=2,'zf'=4,'zn'=4,'y'=4,'core'=2,'plane'=2] {'core'}, dimensions={0}, use_global_device_ids=true | all-gather | bytes 221184 | tf_op jit(solution)/shard_map/all_gather | solution.py:320
  80.5 12.3 %all_to_all.44.got_ref = f32[8,72,128]{2,1,0:T(8,128)S(1)} all-to-all(f32[8,72,128]{2,1,0:T(8,128)S(1)} %shard_map.75), channel_id=1, replica_groups=mesh['x'=2,'zf'=4,'zn'=4,'y'=4,'core'=2,'plane'=2] {'y','plane'}, dimensions={0} | all-to-all | bytes 589824 | tf_op jit(solution)/shard_map/all_to_all | solution.py:317
  92.8 1.1 shard_map.76
  93.9 1.9 %all-gather.3 = f32[128,128]{1,0:T(8,128)S(1)} all-gather(f32[64,128]{1,0:T(8,128)S(1)} %shard_map.76), channel_id=5, replica_groups=mesh['x'=2,'zf'=4,'zn'=4,'y'=4,'core'=2,'plane'=2] {'core'}, dimensions={0}, use_global_device_ids=true | all-gather | bytes 98304 | tf_op jit(solution)/shard_map/all_gather | solution.py:320
  95.8 1.0 shard_map.77
  96.8 11.0 %all_to_all.45.got_ref = f32[8,40,128]{2,1,0:T(8,128)S(1)} all-to-all(f32[8,40,128]{2,1,0:T(8,128)S(1)} %shard_map.77), channel_id=1, replica_groups=mesh['x'=2,'zf'=4,'zn'=4,'y'=4,'core'=2,'plane'=2] {'x','zn'}, dimensions={0} | all-to-all | bytes 327680 | tf_op jit(solution)/shard_map/all_to_all | solution.py:317
  107.8 15.5 %all_to_all.46.got_ref = f32[4,40,128]{2,1,0:T(8,128)S(1)} all-to-all(f32[4,40,128]{2,1,0:T(8,128)S(1)} %shard_map.78), channel_id=1, replica_groups=mesh['x'=2,'zf'=4,'zn'=4,'y'=4,'core'=2,'plane'=2] {'zf'}, dimensions={0} | all-to-all | bytes 163840 | tf_op jit(solution)/shard_map/all_to_all | solution.py:317
  123.3 1.2 shard_map.79
  124.5 10.4 %all_to_all.47 = f32[8,32,128]{2,1,0:T(8,128)S(1)} all-to-all(f32[8,32,128]{2,1,0:T(8,128)S(1)} %shard_map.79), channel_id=1, replica_groups=mesh['x'=2,'zf'=4,'zn'=4,'y'=4,'core'=2,'plane'=2] {'x','zn'}, dimensions={0} | all-to-all | bytes 262144 | tf_op jit(solution)/shard_map/all_to_all | solution.py:317
  135.0 1.2 shard_map.80
  (9 shorter events, 0.1 us)
Async XLA Ops:
  0.6 0.9 copy-start.1
  1.5 0.7 copy-start.2
  2.2 0.7 copy-start.3
  2.8 23.3 %copy-start = (bf16[8,512,256]{2,1,0:T(8,128)(2,1)S(1)}, bf16[8,512,256]{2,1,0:T(8,128)(2,1)}, u32[]{:S(2)}) copy-start(bf16[8,512,256]{2,1,0:T(8,128)(2,1)} %movie_ref.5) | copy-start | bytes 6291460

commit v4 on v3

--- a/solution.py
+++ b/solution.py
@@ -17,9 +17,20 @@
 NP = 8
 LIVE = 64
 ACROSS = ("y", "plane")
-NEAR = ("x", "zn")
-FAR = "zf"
+FRAMES = "tm"
 GRAM = 8
+
+def near_index(device):
+    x, z = device // 16, device % 16
+    a = (z + 2 * (z // 8)) % 4
+    return (a // 2) * 4 + x * 2 + a % 2
+
+
+def near_and_far(count):
+    devices = sorted(range(count), key=lambda i: (i % 16 // 4, near_index(i)))
+    near = [devices[i : i + 8] for i in range(0, count, 8)]
+    return near, [list(group) for group in zip(*near)]
+
 
 VMEM = pl.BlockSpec(memory_space=pltpu.VMEM)
 HBM = pl.BlockSpec(memory_space=pltpu.HBM)
@@ -127,51 +138,52 @@
     return (iota(shape, 0) == neuron).astype(BF16)
 
 
-def first_columns(counts, neuron, foot_ref, traces, first_c_ref, first_a_ref):
-    shape = (KP * NP, KP * NP)
-    q, lane = iota(shape, 0), iota(shape, 1)
+def live_slots(counts, shape):
+    q = iota(shape, 0)
     cnt = jnp.zeros(shape, jnp.int32)
     for p in range(NP):
         cnt = jnp.where(q % NP == p, counts[p], cnt)
-    live = q // NP < cnt
+    return q // NP < cnt
+
+
+def first_traces(counts, neuron, traces_ref):
+    shape = (KP * NP, KP * NP)
+    q, lane = iota(shape, 0), iota(shape, 1)
+    order = (lane == (q % NP) * KP + q // NP).astype(BF16)
+    choose = nt(order, neuron_slots(neuron))
+    half = traces_ref.shape[1] // 2
+    own = traces_ref[:, pl.ds(pl.multiple_of(lax.axis_index("core") * half, half), half)]
+    return jnp.where(live_slots(counts, shape), choose_rows(choose, own), 0.0)
+
+
+def first_footprints(counts, foot_ref):
+    lane = iota((KP * NP, 128), 1)
     half = foot_ref.shape[1] // 2
-    near = lax.axis_index(NEAR)
+    near = near_index(lax.axis_index(FRAMES))
     base = pl.multiple_of((near // 4) * 128, 128)
     turn = 32 * (near % 4)
     first = pltpu.roll(foot_ref[:, pl.ds(base, 128)], (128 - turn) % 128, 1)
     second = pltpu.roll(foot_ref[:, pl.ds(half + base, 128)], (160 - turn) % 128, 1)
     own = jnp.where(lane < 32, first, second)
-    first_a_ref[...] = jnp.where(live & (lane < 64), own, 0.0)
-    order = (lane == (q % NP) * KP + q // NP).astype(BF16)
-    choose = nt(order, neuron_slots(neuron))
-    first_c_ref[...] = jnp.where(live, choose_rows(choose, traces), 0.0)
-
-
-def first_kernel(counts_hbm, neuron_hbm, foot_hbm, traces_hbm, movie_hbm, *refs):
-    out_ref, first_c_ref, first_a_ref, counts_ref, neuron_ref, foot_ref, traces_ref, movie_ref, sems = refs
-    half = traces_ref.shape[1]
-    own = pl.ds(pl.multiple_of(lax.axis_index("core") * half, half), half)
-    pairs = [
-        (counts_hbm, counts_ref),
-        (neuron_hbm, neuron_ref),
-        (foot_hbm, foot_ref),
-        (traces_hbm.at[:, own], traces_ref),
-    ]
+    return jnp.where(live_slots(counts, lane.shape) & (lane < 64), own, 0.0)
+
+
+def first_kernel(counts_hbm, foot_hbm, movie_hbm, out_ref, counts_ref, foot_ref, movie_ref, sems):
+    pairs = [(counts_hbm, counts_ref), (foot_hbm, foot_ref)]
     pairs += [(movie_hbm.at[p], movie_ref.at[p]) for p in range(NP)]
     copies = [pltpu.make_async_copy(src, dst, sems.at[i]) for i, (src, dst) in enumerate(pairs)]
     for copy in copies:
         copy.start()
-    for copy in copies[:4]:
+    for copy in copies[:2]:
         copy.wait()
     counts = spread(counts_ref)
     packed = choose_rows(packer(counts), foot_ref[...])
 
     def movie(p):
-        copies[4 + p].wait()
+        copies[2 + p].wait()
         return movie_ref[p]
 
     project_packed(counts, packed, movie, out_ref)
-    first_columns(counts, neuron_ref[...], foot_ref, traces_ref[...], first_c_ref, first_a_ref)
 
 
 def project_kernel(counts_ref, gathered_ref, movie_ref, out_ref):
@@ -247,6 +259,16 @@
         new_ref[8 * k : 8 * k + 8, :] = xs[k]
 
 
+def first_hals_traces_kernel(counts_ref, neuron_ref, traces_ref, got_ref, out_ref, new_ref, *scratch):
+    new_ref[...] = first_traces(spread(counts_ref), neuron_ref[...], traces_ref)
+    hals_traces_kernel(counts_ref, got_ref, new_ref, out_ref, new_ref, *scratch)
+
+
+def first_hals_footprints_kernel(counts_ref, foot_ref, got_ref, send_ref, new_ref, *scratch):
+    new_ref[...] = first_footprints(spread(counts_ref), foot_ref)
+    hals_footprints_kernel(counts_ref, got_ref, new_ref, send_ref, new_ref, *scratch)
+
+
 def hals_traces_kernel(counts_ref, got_ref, x_ref, out_ref, new_ref, rows, grams, wide):
     counts = spread(counts_ref)
     total = tree_sum([got_ref[j] for j in range(got_ref.shape[0])])
@@ -305,66 +327,63 @@
     )(*args)
 
 
-def local(sizes, movie, footprints, traces, patch_counts, slot_neuron):
-    n_across, n_near, n_far = sizes
+def local(n_across, groups, movie, footprints, traces, patch_counts, slot_neuron):
+    near, far = groups
+    n_near, n_far = len(near[0]), len(far[0])
     slots, patches, voxels = footprints.shape
     q = slots * patches
     foot = footprints.reshape(q, voxels)
     counts = patch_counts.reshape(1, patches)
     neuron = slot_neuron.reshape(1, q)
 
-    def swap(x, axes):
-        return lax.all_to_all(x, axes, 0, 0, tiled=True)
+    def swap(x, axes, members=None):
+        return lax.all_to_all(x, axes, 0, 0, tiled=True, axis_index_groups=members)
 
     def cores(x):
         return lax.all_gather(x, "core", axis=0, tiled=False)
 
     square = pltpu.VMEM((q, 128), F32)
-    state = [(q, 128)]
+    scratch = [square, square, pltpu.VMEM((KP * KP, NP, 128), F32)]
     part = voxels // 2 // n_near
+    half = (LIVE + GRAM, 128)
     for step in range(ITERS):
-        halves = [(2, LIVE + GRAM, 128)]
-        scratch = [square, square, pltpu.VMEM((KP * KP, NP, 128), F32)]
-        if step == ITERS - 1:
-            state, scratch = [], [square] + scratch
         if step == 0:
-            loaded = [counts, neuron, foot, traces, movie]
-            shapes = [counts.shape, neuron.shape, foot.shape, (q, traces.shape[1] // 2), movie.shape]
-            buffers = [pltpu.VMEM(shape, x.dtype) for shape, x in zip(shapes, loaded)]
-            buffers.append(pltpu.SemaphoreType.DMA((4 + patches,)))
-            outs = halves + [(q, 128)] * 2
-            partial, first_c, first_a = call(first_kernel, outs, [HBM] * 5, loaded, buffers, 53.5)
-            x_c, x_a = [first_c], [first_a]
+            loaded = [counts, foot, movie]
+            buffers = [pltpu.VMEM(x.shape, x.dtype) for x in loaded]
+            buffers.append(pltpu.SemaphoreType.DMA((2 + patches,)))
+            (partial,) = call(first_kernel, [(2, *half)], [HBM] * 3, loaded, buffers, 53.8)
         else:
-            (partial,) = call(project_kernel, halves, [], [counts, all_a, movie])
-        (send,) = call(keep_half_kernel, [(n_across, LIVE + GRAM, 128)], [], [cores(partial)])
-        own_c, *x_c = call(
-            hals_traces_kernel, [(LIVE, 128)] + state, [], [counts, swap(send, ACROSS), *x_c], scratch
-        )
+            (partial,) = call(project_kernel, [(2, *half)], [], [counts, all_a, movie])
+        (send,) = call(keep_half_kernel, [(n_across, *half)], [], [cores(partial)])
+        got = swap(send, ACROSS)
+        if step == 0:
+            args = [counts, neuron, traces, got]
+            own_c, x_c = call(first_hals_traces_kernel, [(LIVE, 128), (q, 128)], [], args, scratch)
+        else:
+            (own_c,) = call(hals_traces_kernel, [(LIVE, 128)], [], [counts, got, x_c], [square] + scratch)
         all_c = cores(own_c)
         (send,) = call(correlate_kernel, [(n_near, part + GRAM, 128)], [], [counts, all_c, movie])
-        (send,) = call(keep_part_kernel, [(n_far, part + GRAM, 128)], [], [swap(send, NEAR)])
-        send, *x_a = call(
-            hals_footprints_kernel,
-            [(n_near, part, 128)] + state,
-            [],
-            [counts, swap(send, FAR), *x_a],
-            scratch,
-        )
-        all_a = swap(send, NEAR).reshape(voxels // 2, 128)
+        (send,) = call(keep_part_kernel, [(n_far, part + GRAM, 128)], [], [swap(send, FRAMES, near)])
+        got = swap(send, FRAMES, far)
+        if step == 0:
+            args = [counts, foot, got]
+            send, x_a = call(first_hals_footprints_kernel, [(n_near, part, 128), (q, 128)], [], args, scratch)
+        else:
+            args = [counts, got, x_a]
+            (send,) = call(hals_footprints_kernel, [(n_near, part, 128)], [], args, [square] + scratch)
+        all_a = swap(send, FRAMES, near).reshape(voxels // 2, 128)
     last = [counts, neuron, all_a, all_c, traces]
     new_foot, new_traces = call(last_kernel, [foot.shape, traces.shape], [], last)
     return new_foot.reshape(footprints.shape), new_traces
 
 
 def solution(mesh):
-    names = ("x", "zf", "zn", "y", "core", "plane")
-    shape = (2, mesh.shape["tm"] // 8, 4, mesh.shape["tile"] // 2, 2, mesh.shape["plane"])
+    names = (FRAMES, "y", "core", "plane")
+    shape = (mesh.shape["tm"], mesh.shape["tile"] // 2, 2, mesh.shape["plane"])
     fine = jax.sharding.Mesh(mesh.devices.reshape(shape), names)
-    frames, voxels = names[:3], names[3:]
-    sizes = (shape[3] * shape[5], shape[0] * shape[2], shape[1])
+    frames, voxels = FRAMES, names[1:]
     return jax.shard_map(
-        functools.partial(local, sizes),
+        functools.partial(local, shape[1] * shape[3], near_and_far(shape[0])),
         mesh=fine,
         in_specs=(P(None, voxels, frames), P(None, None, voxels), P(None, frames), P(), P()),
         out_specs=(P(None, None, voxels), P(None, frames)),

time: 137 us -> 130 us (0.949)
  the two profiles are of different devices: /device:TPU:2 before, /device:TPU:8 now
where the time goes in v4:
time: 130 us
  blocking collectives  117 us (90%)
  Pallas kernels  11.6 us (9%)
    all_to_all x8, blocking collectives, swap(): return lax.all_to_all(x, axes, 0, 0, tiled=True, axis_index_groups=members)  109 us
    pallas_call x13, Pallas kernels, call(): pl.pallas_call(kernel, out_shape=[jax.ShapeDtypeStruct(s, F32) for s in o...  11.6 us
    all_gather x4, blocking collectives, cores(): return lax.all_gather(x, 'core', axis=0, tiled=False)  7.6 us

profile of v4, /device:TPU:8, one launch (start us, length us, event | category | flops | bytes accessed | tf_op | source)
XLA Modules:
  0.0 130.0 jit_solution(15419878291285055246)
XLA Ops:
  0.7 0.7 copy-done.3
  1.3 2.7 %shard_map.68 = f32[2,72,128]{2,1,0:T(8,128)S(1)} custom-call(s32[1,8]{1,0:T(1,128)S(1)} %bitcast.19, f32[128,512]{1,0:T(8,128)} %bitcast.10, bf16[8,512,256]{2,1,0:T(8,128)(2,1)} %movie_ref.5), custom_call_target="tpu_custom_call" | custom-call | tf_op jit(solution)/shard_map/pallas_call | solution.py:320
  4.1 1.9 %all-gather = f32[4,72,128]{2,1,0:T(8,128)S(1)} all-gather(f32[2,72,128]{2,1,0:T(8,128)S(1)} %shard_map.68), channel_id=2, replica_groups=mesh['tm'=32,'y'=4,'core'=2,'plane'=2] {'core'}, dimensions={0}, use_global_device_ids=true | all-gather | bytes 221184 | tf_op jit(solution)/shard_map/all_gather | solution.py:343
  6.0 0.0 copy-start.1
  6.0 16.8 %all_to_all.40.got_ref = f32[8,72,128]{2,1,0:T(8,128)S(1)} all-to-all(f32[8,72,128]{2,1,0:T(8,128)S(1)} %shard_map.69), channel_id=1, replica_groups=mesh['tm'=32,'y'=4,'core'=2,'plane'=2] {'y','plane'}, dimensions={0} | all-to-all | bytes 589824 | tf_op jit(solution)/shard_map/all_to_all | solution.py:340
  22.9 0.0 copy-done.4
  22.9 1.1 shard_map.70
  24.0 1.9 %all-gather.1 = f32[128,128]{1,0:T(8,128)S(1)} all-gather(f32[64,128]{1,0:T(8,128)S(1)} %get-tuple-element.8), channel_id=3, replica_groups=mesh['tm'=32,'y'=4,'core'=2,'plane'=2] {'core'}, dimensions={0}, use_global_device_ids=true | all-gather | bytes 98304 | tf_op jit(solution)/shard_map/all_gather | solution.py:343
  25.8 1.0 shard_map.71
  26.9 12.2 %all_to_all.41.got_ref = f32[8,40,128]{2,1,0:T(8,128)S(1)} all-to-all(f32[8,40,128]{2,1,0:T(8,128)S(1)} %shard_map.71), channel_id=1, replica_groups={{0,16,256,272,32,48,288,304},{64,80,320,336,96,112,352,368},{160,176,41..., dimensions={0} | all-to-all | bytes 327680 | tf_op jit(solution)/shard_map/all_to_all | solution.py:340
  39.1 21.4 %all_to_all.42.got_ref = f32[4,40,128]{2,1,0:T(8,128)S(1)} all-to-all(f32[4,40,128]{2,1,0:T(8,128)S(1)} %shard_map.72), channel_id=1, replica_groups={{0,64,160,224},{16,80,176,240},{256,320,416,480},{272,336,432,496},{32,..., dimensions={0} | all-to-all | bytes 163840 | tf_op jit(solution)/shard_map/all_to_all | solution.py:340
  60.5 1.3 shard_map.73
  61.8 11.2 %all_to_all.43 = f32[8,32,128]{2,1,0:T(8,128)S(1)} all-to-all(f32[8,32,128]{2,1,0:T(8,128)S(1)} %get-tuple-element.9), channel_id=1, replica_groups={{0,16,256,272,32,48,288,304},{64,80,320,336,96,112,352,368},{160,176,41..., dimensions={0} | all-to-all | bytes 262144 | tf_op jit(solution)/shard_map/all_to_all | solution.py:340
  73.0 0.7 shard_map.74
  73.8 2.0 %all-gather.2 = f32[4,72,128]{2,1,0:T(8,128)S(1)} all-gather(f32[2,72,128]{2,1,0:T(8,128)S(1)} %shard_map.74), channel_id=4, replica_groups=mesh['tm'=32,'y'=4,'core'=2,'plane'=2] {'core'}, dimensions={0}, use_global_device_ids=true | all-gather | bytes 221184 | tf_op jit(solution)/shard_map/all_gather | solution.py:343
  75.8 12.5 %all_to_all.44.got_ref = f32[8,72,128]{2,1,0:T(8,128)S(1)} all-to-all(f32[8,72,128]{2,1,0:T(8,128)S(1)} %shard_map.75), channel_id=1, replica_groups=mesh['tm'=32,'y'=4,'core'=2,'plane'=2] {'y','plane'}, dimensions={0} | all-to-all | bytes 589824 | tf_op jit(solution)/shard_map/all_to_all | solution.py:340
  88.2 1.1 shard_map.76
  89.3 1.9 %all-gather.3 = f32[128,128]{1,0:T(8,128)S(1)} all-gather(f32[64,128]{1,0:T(8,128)S(1)} %shard_map.76), channel_id=5, replica_groups=mesh['tm'=32,'y'=4,'core'=2,'plane'=2] {'core'}, dimensions={0}, use_global_device_ids=true | all-gather | bytes 98304 | tf_op jit(solution)/shard_map/all_gather | solution.py:343
  91.2 1.0 shard_map.77
  92.3 10.5 %all_to_all.45.got_ref = f32[8,40,128]{2,1,0:T(8,128)S(1)} all-to-all(f32[8,40,128]{2,1,0:T(8,128)S(1)} %shard_map.77), channel_id=1, replica_groups={{0,16,256,272,32,48,288,304},{64,80,320,336,96,112,352,368},{160,176,41..., dimensions={0} | all-to-all | bytes 327680 | tf_op jit(solution)/shard_map/all_to_all | solution.py:340
  102.7 15.0 %all_to_all.46.got_ref = f32[4,40,128]{2,1,0:T(8,128)S(1)} all-to-all(f32[4,40,128]{2,1,0:T(8,128)S(1)} %shard_map.78), channel_id=1, replica_groups={{0,64,160,224},{16,80,176,240},{256,320,416,480},{272,336,432,496},{32,..., dimensions={0} | all-to-all | bytes 163840 | tf_op jit(solution)/shard_map/all_to_all | solution.py:340
  117.7 1.2 shard_map.79
  119.0 9.7 %all_to_all.47 = f32[8,32,128]{2,1,0:T(8,128)S(1)} all-to-all(f32[8,32,128]{2,1,0:T(8,128)S(1)} %shard_map.79), channel_id=1, replica_groups={{0,16,256,272,32,48,288,304},{64,80,320,336,96,112,352,368},{160,176,41..., dimensions={0} | all-to-all | bytes 262144 | tf_op jit(solution)/shard_map/all_to_all | solution.py:340
  128.7 1.2 shard_map.80
  (11 shorter events, 0.1 us)
Async XLA Ops:
  0.6 22.2 %copy-start.2 = (f32[128,256]{1,0:T(8,128)S(1)}, f32[128,256]{1,0:T(8,128)}, u32[]{:S(2)}) copy-start(f32[128,256]{1,0:T(8,128)} %traces_ref.3) | copy-start | bytes 393220
  0.6 0.7 copy-start.3
  1.3 21.5 %copy-start.4 = (s32[128]{0:T(128)S(1)}, s32[128]{0:T(128)}, u32[]{:S(2)}) copy-start(s32[128]{0:T(128)} %param.9) | copy-start | bytes 1540
  1.3 24.5 %copy-start = (bf16[8,512,256]{2,1,0:T(8,128)(2,1)S(1)}, bf16[8,512,256]{2,1,0:T(8,128)(2,1)}, u32[]{:S(2)}) copy-start(bf16[8,512,256]{2,1,0:T(8,128)(2,1)} %movie_ref.5) | copy-start | bytes 6291460
  6.0 54.5 %copy-start.1 = (f32[16,8,512]{2,1,0:T(8,128)S(1)}, f32[16,8,512]{2,1,0:T(8,128)}, u32[]{:S(2)}) copy-start(f32[16,8,512]{2,1,0:T(8,128)} %param.6) | copy-start | bytes 786436

commit v5 on v4

--- a/solution.py
+++ b/solution.py
@@ -23,13 +23,13 @@
 def near_index(device):
     x, z = device // 16, device % 16
     a = (z + 2 * (z // 8)) % 4
-    return (a // 2) * 4 + x * 2 + a % 2
+    return a * 2 + x
 
 
 def near_and_far(count):
     devices = sorted(range(count), key=lambda i: (i % 16 // 4, near_index(i)))
     near = [devices[i : i + 8] for i in range(0, count, 8)]
-    return near, [list(group) for group in zip(*near)]
+    return near, [[g[0], g[2], g[1], g[3]] for g in zip(*near)]
 
 
 VMEM = pl.BlockSpec(memory_space=pltpu.VMEM)
@@ -119,7 +119,7 @@
     return jnp.concatenate([by_slot[:8], by_slot[8:]], axis=1)
 
 
-def project_packed(counts, packed, movie, out_ref):
+def project_packed(counts, packed, movie):
     low = packed.astype(BF16)
     patch, _ = patch_and_slot(counts, low.shape, 0)
     zero = jnp.zeros_like(low)
@@ -128,9 +128,7 @@
         term = nn(jnp.where(patch == p, low, zero), movie(p))
         total = term if p == 0 else total + term
     gram = gram_chunk(counts, nt(packed, packed, precision=HIGH))
-    for h in range(2):
-        out_ref[h, :LIVE, :] = total[:, 128 * h : 128 * h + 128]
-        out_ref[h, LIVE:, :] = gram
+    return [total[:, :128], total[:, 128:]], gram
 
 
 def neuron_slots(neuron):
@@ -142,18 +140,16 @@
     q = iota(shape, 0)
     cnt = jnp.zeros(shape, jnp.int32)
     for p in range(NP):
-        cnt = jnp.where(q % NP == p, counts[p], cnt)
+        cnt = jnp.where(q % NP == p, fit(counts[p], shape), cnt)
     return q // NP < cnt
 
 
-def first_traces(counts, neuron, traces_ref):
+def first_traces(counts, neuron, traces):
     shape = (KP * NP, KP * NP)
     q, lane = iota(shape, 0), iota(shape, 1)
     order = (lane == (q % NP) * KP + q // NP).astype(BF16)
     choose = nt(order, neuron_slots(neuron))
-    half = traces_ref.shape[1] // 2
-    own = traces_ref[:, pl.ds(pl.multiple_of(lax.axis_index("core") * half, half), half)]
-    return jnp.where(live_slots(counts, shape), choose_rows(choose, own), 0.0)
+    return jnp.where(live_slots(counts, traces.shape), choose_rows(choose, traces), 0.0)
 
 
 def first_footprints(counts, foot_ref):
@@ -183,14 +179,21 @@
         copies[2 + p].wait()
         return movie_ref[p]
 
-    project_packed(counts, packed, movie, out_ref)
+    halves, gram = project_packed(counts, packed, movie)
+    for h in range(2):
+        out_ref[h, :LIVE, :] = halves[h]
+        out_ref[h, LIVE:, :] = gram
 
 
 def project_kernel(counts_ref, gathered_ref, movie_ref, out_ref):
     counts = spread(counts_ref)
     rows = jnp.concatenate([gathered_ref[:128].T, gathered_ref[128:].T], axis=1)
     packed = jnp.concatenate([rows[:LIVE], rows[LIVE:]], axis=1)
-    project_packed(counts, packed, lambda p: movie_ref[p], out_ref)
+    halves, gram = project_packed(counts, packed, lambda p: movie_ref[p])
+    for j in range(out_ref.shape[0]):
+        for h in range(2):
+            out_ref[j, LIVE * h : LIVE * h + LIVE, :] = halves[h]
+        out_ref[j, 2 * LIVE :, :] = gram
 
 
 def keep_half_kernel(got_ref, send_ref):
@@ -200,15 +203,19 @@
         send_ref[j] = kept
 
 
+def add_kernel(got_ref, out_ref):
+    out_ref[...] = tree_sum([got_ref[j] for j in range(got_ref.shape[0])])
+
+
 def keep_part_kernel(got_ref, send_ref):
     total = tree_sum([got_ref[j] for j in range(got_ref.shape[0])])
     for j in range(send_ref.shape[0]):
         send_ref[j] = total
 
 
-def correlate_kernel(counts_ref, gathered_ref, movie_ref, send_ref):
-    counts = spread(counts_ref)
-    rows = jnp.concatenate([gathered_ref[0], gathered_ref[1]], axis=1)
+def correlate_kernel(counts_ref, rows_ref, movie_ref, send_ref):
+    counts = spread(counts_ref)
+    rows = rows_ref[...]
     gram = gram_chunk(counts, nt(rows, rows, precision=HIGH))
     low = rows.T.astype(BF16)
     patch, _ = patch_and_slot(counts, low.shape, 1)
@@ -235,32 +242,31 @@
 
 def hals(target, gram, x_ref, new_ref, wide):
     shape = (NP, 128)
+    blocks = range(0, x_ref.shape[1], 128)
     for k in range(KP):
-        own = gram(k)
+        own = gram[8 * k : 8 * k + 8, :KP]
         scale = 1.0 / (jnp.broadcast_to(own[:, k : k + 1], shape) + RIDGE)
         for t in range(KP):
-            entry = jnp.broadcast_to(own[:, t : t + 1], shape)
-            wide[KP * k + t] = entry * scale
-        wide[KP * k + k] = target(k) * scale
-
-    def sweep(_, xs):
-        xs = list(xs)
+            if t != k:
+                wide[KP * k + t] = jnp.broadcast_to(own[:, t : t + 1], shape) * scale
+        for at in blocks:
+            target[8 * k : 8 * k + 8, at : at + 128] = target[8 * k : 8 * k + 8, at : at + 128] * scale
+    xs = [[x_ref[8 * k : 8 * k + 8, at : at + 128] for k in range(KP)] for at in blocks]
+    for _ in range(SWEEPS):
         for k in range(KP):
-            terms = [wide[KP * k + t] * xs[t] for t in range(KP) if t != k]
-            last = terms.pop(k - 1 if k else KP - 2)
-            rest = wide[KP * k + k] - tree_sum(terms)
-            xs[k] = jnp.maximum(rest - last, 0.0)
-        return tuple(xs)
-
-    xs = tuple(x_ref[8 * k : 8 * k + 8, :] for k in range(KP))
-    for sweep_index in range(SWEEPS):
-        xs = sweep(sweep_index, xs)
-    for k in range(KP):
-        new_ref[8 * k : 8 * k + 8, :] = xs[k]
+            weights = [wide[KP * k + t] for t in range(KP) if t != k]
+            for at, x in zip(blocks, xs):
+                terms = [w * x[t] for w, t in zip(weights, [t for t in range(KP) if t != k])]
+                last = terms.pop(k - 1 if k else KP - 2)
+                rest = target[8 * k : 8 * k + 8, at : at + 128] - tree_sum(terms)
+                x[k] = jnp.maximum(rest - last, 0.0)
+    for at, x in zip(blocks, xs):
+        for k in range(KP):
+            new_ref[8 * k : 8 * k + 8, at : at + 128] = x[k]
 
 
 def first_hals_traces_kernel(counts_ref, neuron_ref, traces_ref, got_ref, out_ref, new_ref, *scratch):
-    new_ref[...] = first_traces(spread(counts_ref), neuron_ref[...], traces_ref)
+    new_ref[...] = first_traces(spread(counts_ref), neuron_ref[...], traces_ref[...])
     hals_traces_kernel(counts_ref, got_ref, new_ref, out_ref, new_ref, *scratch)
 
 
@@ -271,13 +277,16 @@
 
 def hals_traces_kernel(counts_ref, got_ref, x_ref, out_ref, new_ref, rows, grams, wide):
     counts = spread(counts_ref)
-    total = tree_sum([got_ref[j] for j in range(got_ref.shape[0])])
+    if got_ref.shape[1] == LIVE + GRAM:
+        halves, gram = [got_ref[0, :LIVE], got_ref[1, :LIVE]], got_ref[0, LIVE:]
+    else:
+        total = got_ref[0] + got_ref[1]
+        halves, gram = [total[:LIVE], total[LIVE : 2 * LIVE]], total[2 * LIVE :]
     unpack = unpacker(counts)
-    gram = total[LIVE:]
     gram = jnp.concatenate([gram[:, :LIVE], gram[:, LIVE:]], axis=0)
-    rows[...] = choose_rows(unpack, total[:LIVE])
+    rows[...] = choose_rows(unpack, jnp.concatenate(halves, axis=1))
     grams[:, :KP] = choose_cols(unpack, gram)
-    hals(lambda k: rows[8 * k : 8 * k + 8, :], lambda k: grams[8 * k : 8 * k + 8, :KP], x_ref, new_ref, wide)
+    hals(rows, grams, x_ref, new_ref, wide)
     out_ref[...] = choose_rows(packer(counts), new_ref[...])
 
 
@@ -292,7 +301,7 @@
     rows[:, : 2 * size] = choose_cols(unpack, cols)
     rows[:, 2 * size :] = jnp.zeros((KP * NP, 128 - 2 * size), F32)
     grams[:, :KP] = choose_cols(unpack, gram)
-    hals(lambda k: rows[8 * k : 8 * k + 8, :], lambda k: grams[8 * k : 8 * k + 8, :KP], x_ref, new_ref, wide)
+    hals(rows, grams, x_ref, new_ref, wide)
     packed = choose_rows(packer(counts), new_ref[...]).T
     chunk = jnp.concatenate([packed[:size], packed[size : 2 * size]], axis=1)
     for j in range(send_ref.shape[0]):
@@ -306,9 +315,7 @@
     kept = (iota(shape, 1) == patch * KP + slot).astype(BF16)
     place = nt(neuron_slots(neuron_ref[...]), kept)
     live = jnp.sum(place, axis=1, keepdims=True) > 0.5
-    for h in range(2):
-        at = slice(128 * h, 128 * h + 128)
-        out_ref[:, at] = jnp.where(live, choose_rows(place, all_c_ref[h]), traces_ref[:, at])
+    out_ref[...] = jnp.where(live, choose_rows(place, all_c_ref[...]), traces_ref[...])
     half = all_a_ref.shape[0]
     unpack = unpacker(counts)
     all_a = all_a_ref[...]
@@ -339,38 +346,45 @@
     def swap(x, axes, members=None):
         return lax.all_to_all(x, axes, 0, 0, tiled=True, axis_index_groups=members)
 
+    def hals_scratch(columns):
+        return [pltpu.VMEM((q, columns), F32), pltpu.VMEM((q, 128), F32), pltpu.VMEM((KP * KP, NP, 128), F32)]
+
+    frames = traces.shape[1]
+    part = voxels // 2 // n_near
+    half, whole = (LIVE + GRAM, 128), (2 * LIVE + GRAM, 128)
+
     def cores(x):
         return lax.all_gather(x, "core", axis=0, tiled=False)
 
-    square = pltpu.VMEM((q, 128), F32)
-    scratch = [square, square, pltpu.VMEM((KP * KP, NP, 128), F32)]
-    part = voxels // 2 // n_near
-    half = (LIVE + GRAM, 128)
     for step in range(ITERS):
         if step == 0:
             loaded = [counts, foot, movie]
             buffers = [pltpu.VMEM(x.shape, x.dtype) for x in loaded]
             buffers.append(pltpu.SemaphoreType.DMA((2 + patches,)))
-            (partial,) = call(first_kernel, [(2, *half)], [HBM] * 3, loaded, buffers, 53.8)
+            (both,) = call(first_kernel, [(2, *half)], [HBM] * 3, loaded, buffers, 53.8)
+            (send,) = call(keep_half_kernel, [(n_across, *half)], [], [cores(both)])
         else:
-            (partial,) = call(project_kernel, [(2, *half)], [], [counts, all_a, movie])
-        (send,) = call(keep_half_kernel, [(n_across, *half)], [], [cores(partial)])
-        got = swap(send, ACROSS)
+            (send,) = call(project_kernel, [(n_across, *whole)], [], [counts, all_a, movie])
+        (added,) = call(add_kernel, [send.shape[1:]], [], [swap(send, ACROSS)])
+        got = cores(added)
+        scratch = hals_scratch(frames)
+        outs = [(LIVE, frames), (q, frames)]
         if step == 0:
-            args = [counts, neuron, traces, got]
-            own_c, x_c = call(first_hals_traces_kernel, [(LIVE, 128), (q, 128)], [], args, scratch)
+            all_c, x_c = call(first_hals_traces_kernel, outs, [], [counts, neuron, traces, got], scratch)
         else:
-            (own_c,) = call(hals_traces_kernel, [(LIVE, 128)], [], [counts, got, x_c], [square] + scratch)
-        all_c = cores(own_c)
+            new = pltpu.VMEM((q, frames), F32)
+            (all_c,) = call(hals_traces_kernel, outs[:1], [], [counts, got, x_c], [new] + scratch)
         (send,) = call(correlate_kernel, [(n_near, part + GRAM, 128)], [], [counts, all_c, movie])
         (send,) = call(keep_part_kernel, [(n_far, part + GRAM, 128)], [], [swap(send, FRAMES, near)])
         got = swap(send, FRAMES, far)
+        scratch = hals_scratch(128)
         if step == 0:
             args = [counts, foot, got]
             send, x_a = call(first_hals_footprints_kernel, [(n_near, part, 128), (q, 128)], [], args, scratch)
         else:
             args = [counts, got, x_a]
-            (send,) = call(hals_footprints_kernel, [(n_near, part, 128)], [], args, [square] + scratch)
+            new = pltpu.VMEM((q, 128), F32)
+            (send,) = call(hals_footprints_kernel, [(n_near, part, 128)], [], args, [new] + scratch)
         all_a = swap(send, FRAMES, near).reshape(voxels // 2, 128)
     last = [counts, neuron, all_a, all_c, traces]
     new_foot, new_traces = call(last_kernel, [foot.shape, traces.shape], [], last)

time: 130 us -> 129 us (level)
  blocking collectives: 117 us -> 115 us
    all_gather x4 -> x3, blocking collectives: 7.6 us -> 5.68 us  [cores(): return lax.all_gather(x, 'core', axis=0, tiled=False)]
    pallas_call x13 -> x14, Pallas kernels: 11.6 us -> 11.9 us  [call(): pl.pallas_call(kernel, out_shape=[jax.ShapeDtypeStruct(s, F32) for s in o...]
where the time goes in v5:
time: 129 us; the launch traced here: 128 us
  blocking collectives  115 us (89%)
  Pallas kernels  11.9 us (9%)
    all_to_all x8, blocking collectives, swap(): return lax.all_to_all(x, axes, 0, 0, tiled=True, axis_index_groups=members)  109 us
    pallas_call x14, Pallas kernels, call(): pl.pallas_call(kernel, out_shape=[jax.ShapeDtypeStruct(s, F32) for s in o...  11.9 us
    all_gather x3, blocking collectives, cores(): return lax.all_gather(x, 'core', axis=0, tiled=False)  5.68 us

profile of v5, /device:TPU:8, one launch (start us, length us, event | category | flops | bytes accessed | tf_op | source)
XLA Modules:
  0.0 128.5 jit_solution(11761125698300006058)
XLA Ops:
  0.6 0.0 copy-start.2
  0.7 0.7 copy-done.3
  1.3 2.7 %shard_map.68 = f32[2,72,128]{2,1,0:T(8,128)S(1)} custom-call(s32[1,8]{1,0:T(1,128)S(1)} %bitcast.16, f32[128,512]{1,0:T(8,128)} %bitcast.9, bf16[8,512,256]{2,1,0:T(8,128)(2,1)} %movie_ref.5), custom_call_target="tpu_custom_call" | custom-call | tf_op jit(solution)/shard_map/pallas_call | solution.py:327
  4.1 1.9 %all-gather = f32[4,72,128]{2,1,0:T(8,128)S(1)} all-gather(f32[2,72,128]{2,1,0:T(8,128)S(1)} %shard_map.68), channel_id=2, replica_groups=mesh['tm'=32,'y'=4,'core'=2,'plane'=2] {'core'}, dimensions={0}, use_global_device_ids=true | all-gather | bytes 221184 | tf_op jit(solution)/shard_map/all_gather | solution.py:357
  6.0 0.0 copy-start.1
  6.0 16.8 %all_to_all.40.got_ref = f32[8,72,128]{2,1,0:T(8,128)S(1)} all-to-all(f32[8,72,128]{2,1,0:T(8,128)S(1)} %shard_map.69), channel_id=1, replica_groups=mesh['tm'=32,'y'=4,'core'=2,'plane'=2] {'y','plane'}, dimensions={0} | all-to-all | bytes 589824 | tf_op jit(solution)/shard_map/all_to_all | solution.py:347
  22.9 1.9 %all-gather.1 = f32[144,128]{1,0:T(8,128)S(1)} all-gather(f32[72,128]{1,0:T(8,128)S(1)} %shard_map.70), channel_id=3, replica_groups=mesh['tm'=32,'y'=4,'core'=2,'plane'=2] {'core'}, dimensions={0}, use_global_device_ids=true | all-gather | bytes 110592 | tf_op jit(solution)/shard_map/all_gather | solution.py:357
  24.7 1.3 shard_map.71
  26.0 0.0 copy-done
  26.0 1.0 shard_map.72
  27.1 12.2 %all_to_all.41.got_ref = f32[8,40,128]{2,1,0:T(8,128)S(1)} all-to-all(f32[8,40,128]{2,1,0:T(8,128)S(1)} %shard_map.72), channel_id=1, replica_groups={{0,256,16,272,32,288,48,304},{64,320,80,336,96,352,112,368},{160,416,17..., dimensions={0} | all-to-all | bytes 327680 | tf_op jit(solution)/shard_map/all_to_all | solution.py:347
  39.3 20.5 %all_to_all.42.got_ref = f32[4,40,128]{2,1,0:T(8,128)S(1)} all-to-all(f32[4,40,128]{2,1,0:T(8,128)S(1)} %shard_map.73), channel_id=1, replica_groups={{0,160,64,224},{256,416,320,480},{16,176,80,240},{272,432,336,496},{32,..., dimensions={0} | all-to-all | bytes 163840 | tf_op jit(solution)/shard_map/all_to_all | solution.py:347
  59.8 1.2 shard_map.74
  61.1 11.2 %all_to_all.43 = f32[8,32,128]{2,1,0:T(8,128)S(1)} all-to-all(f32[8,32,128]{2,1,0:T(8,128)S(1)} %get-tuple-element.9), channel_id=1, replica_groups={{0,256,16,272,32,288,48,304},{64,320,80,336,96,352,112,368},{160,416,17..., dimensions={0} | all-to-all | bytes 262144 | tf_op jit(solution)/shard_map/all_to_all | solution.py:347
  72.3 0.7 shard_map.75
  73.1 13.5 %all_to_all.44.got_ref = f32[8,136,128]{2,1,0:T(8,128)S(1)} all-to-all(f32[8,136,128]{2,1,0:T(8,128)S(1)} %shard_map.75), channel_id=1, replica_groups=mesh['tm'=32,'y'=4,'core'=2,'plane'=2] {'y','plane'}, dimensions={0} | all-to-all | bytes 1114112 | tf_op jit(solution)/shard_map/all_to_all | solution.py:347
  86.5 1.9 %all-gather.2 = f32[272,128]{1,0:T(8,128)S(1)} all-gather(f32[136,128]{1,0:T(8,128)S(1)} %shard_map.76), channel_id=4, replica_groups=mesh['tm'=32,'y'=4,'core'=2,'plane'=2] {'core'}, dimensions={0}, use_global_device_ids=true | all-gather | bytes 208896 | tf_op jit(solution)/shard_map/all_gather | solution.py:357
  88.4 1.2 shard_map.77.rows_ref.all_c_ref
  89.7 1.1 shard_map.78
  90.8 10.5 %all_to_all.45.got_ref = f32[8,40,128]{2,1,0:T(8,128)S(1)} all-to-all(f32[8,40,128]{2,1,0:T(8,128)S(1)} %shard_map.78), channel_id=1, replica_groups={{0,256,16,272,32,288,48,304},{64,320,80,336,96,352,112,368},{160,416,17..., dimensions={0} | all-to-all | bytes 327680 | tf_op jit(solution)/shard_map/all_to_all | solution.py:347
  101.2 14.7 %all_to_all.46.got_ref = f32[4,40,128]{2,1,0:T(8,128)S(1)} all-to-all(f32[4,40,128]{2,1,0:T(8,128)S(1)} %shard_map.79), channel_id=1, replica_groups={{0,160,64,224},{256,416,320,480},{16,176,80,240},{272,432,336,496},{32,..., dimensions={0} | all-to-all | bytes 163840 | tf_op jit(solution)/shard_map/all_to_all | solution.py:347
  116.0 1.2 shard_map.80
  117.2 10.0 %all_to_all.47 = f32[8,32,128]{2,1,0:T(8,128)S(1)} all-to-all(f32[8,32,128]{2,1,0:T(8,128)S(1)} %shard_map.80), channel_id=1, replica_groups={{0,256,16,272,32,288,48,304},{64,320,80,336,96,352,112,368},{160,416,17..., dimensions={0} | all-to-all | bytes 262144 | tf_op jit(solution)/shard_map/all_to_all | solution.py:347
  127.2 1.2 shard_map.81
  (11 shorter events, 0.1 us)
Async XLA Ops:
  0.6 24.1 %copy-start.2 = (f32[128,256]{1,0:T(8,128)S(1)}, f32[128,256]{1,0:T(8,128)}, u32[]{:S(2)}) copy-start(f32[128,256]{1,0:T(8,128)} %traces_ref.3) | copy-start | bytes 393220
  0.6 0.7 copy-start.3
  1.3 23.4 %copy-start.4 = (s32[128]{0:T(128)S(1)}, s32[128]{0:T(128)}, u32[]{:S(2)}) copy-start(s32[128]{0:T(128)} %param.9) | copy-start | bytes 1540
  1.3 24.7 %copy-start = (bf16[8,512,256]{2,1,0:T(8,128)(2,1)S(1)}, bf16[8,512,256]{2,1,0:T(8,128)(2,1)}, u32[]{:S(2)}) copy-start(bf16[8,512,256]{2,1,0:T(8,128)(2,1)} %movie_ref.5) | copy-start | bytes 6291460
  6.0 53.8 %copy-start.1 = (f32[16,8,512]{2,1,0:T(8,128)S(1)}, f32[16,8,512]{2,1,0:T(8,128)}, u32[]{:S(2)}) copy-start(f32[16,8,512]{2,1,0:T(8,128)} %param.6) | copy-start | bytes 786436

commit v6 on v5

--- a/solution.py
+++ b/solution.py
@@ -10,13 +10,13 @@
 ITERS = 2
 SWEEPS = 3
 RIDGE = 1.0
-HIGH = lax.Precision.HIGHEST
 F32 = jnp.float32
 BF16 = jnp.bfloat16
 KP = 16
 NP = 8
 LIVE = 64
-ACROSS = ("y", "plane")
+VOXELS = ("y", "core", "plane")
+ACROSS = [(0, 0), (2, 1), (1, 0), (3, 1), (2, 0), (0, 1), (3, 0), (1, 1)]
 FRAMES = "tm"
 GRAM = 8
 
@@ -65,6 +65,11 @@
 
 def fit(row, shape):
     return row[:, : shape[1]] if shape[1] <= 128 else jnp.concatenate([row] * (shape[1] // 128), axis=1)
+
+
+def products(rows):
+    high, low, _ = split(rows)
+    return nt(jnp.concatenate([high, low, high], axis=1), jnp.concatenate([high, high, low], axis=1))
 
 
 def offsets(counts, shape):
@@ -127,7 +132,7 @@
     for p in range(NP):
         term = nn(jnp.where(patch == p, low, zero), movie(p))
         total = term if p == 0 else total + term
-    gram = gram_chunk(counts, nt(packed, packed, precision=HIGH))
+    gram = gram_chunk(counts, products(packed))
     return [total[:, :128], total[:, 128:]], gram
 
 
@@ -216,7 +221,7 @@
 def correlate_kernel(counts_ref, rows_ref, movie_ref, send_ref):
     counts = spread(counts_ref)
     rows = rows_ref[...]
-    gram = gram_chunk(counts, nt(rows, rows, precision=HIGH))
+    gram = gram_chunk(counts, products(rows))
     low = rows.T.astype(BF16)
     patch, _ = patch_and_slot(counts, low.shape, 1)
     zero = jnp.zeros_like(low)
@@ -336,6 +341,7 @@
 
 def local(n_across, groups, movie, footprints, traces, patch_counts, slot_neuron):
     near, far = groups
+    across = [[4 * y + 2 * core + p for y, p in ACROSS] for core in range(2)]
     n_near, n_far = len(near[0]), len(far[0])
     slots, patches, voxels = footprints.shape
     q = slots * patches
@@ -365,7 +371,7 @@
             (send,) = call(keep_half_kernel, [(n_across, *half)], [], [cores(both)])
         else:
             (send,) = call(project_kernel, [(n_across, *whole)], [], [counts, all_a, movie])
-        (added,) = call(add_kernel, [send.shape[1:]], [], [swap(send, ACROSS)])
+        (added,) = call(add_kernel, [send.shape[1:]], [], [swap(send, VOXELS, across)])
         got = cores(added)
         scratch = hals_scratch(frames)
         outs = [(LIVE, frames), (q, frames)]

time: 129 us -> 129 us (level)
  no operation moved by 1% of the time
where the time goes in v6:
time: 129 us; the launch traced here: 128 us
  blocking collectives  115 us (89%)
  Pallas kernels  11.6 us (9%)
    all_to_all x8, blocking collectives, swap(): return lax.all_to_all(x, axes, 0, 0, tiled=True, axis_index_groups=members)  109 us
    pallas_call x14, Pallas kernels, call(): pl.pallas_call(kernel, out_shape=[jax.ShapeDtypeStruct(s, F32) for s in o...  11.6 us
    all_gather x3, blocking collectives, cores(): return lax.all_gather(x, 'core', axis=0, tiled=False)  5.68 us

profile of v6, /device:TPU:8, one launch (start us, length us, event | category | flops | bytes accessed | tf_op | source)
XLA Modules:
  0.0 128.1 jit_solution(16501812617888517887)
XLA Ops:
  0.7 0.7 copy-done.3
  1.3 2.6 %shard_map.68 = f32[2,72,128]{2,1,0:T(8,128)S(1)} custom-call(s32[1,8]{1,0:T(1,128)S(1)} %bitcast.16, f32[128,512]{1,0:T(8,128)} %bitcast.9, bf16[8,512,256]{2,1,0:T(8,128)(2,1)} %movie_ref.5), custom_call_target="tpu_custom_call" | custom-call | tf_op jit(solution)/shard_map/pallas_call | solution.py:332
  4.0 1.9 %all-gather = f32[4,72,128]{2,1,0:T(8,128)S(1)} all-gather(f32[2,72,128]{2,1,0:T(8,128)S(1)} %shard_map.68), channel_id=2, replica_groups=mesh['tm'=32,'y'=4,'core'=2,'plane'=2] {'core'}, dimensions={0}, use_global_device_ids=true | all-gather | bytes 221184 | tf_op jit(solution)/shard_map/all_gather | solution.py:363
  5.9 0.0 copy-start.1
  5.9 16.8 %all_to_all.40.got_ref = f32[8,72,128]{2,1,0:T(8,128)S(1)} all-to-all(f32[8,72,128]{2,1,0:T(8,128)S(1)} %shard_map.69), channel_id=1, replica_groups={{0,9,4,13,8,1,12,5},{2,11,6,15,10,3,14,7},{16,25,20,29,24,17,28,21},{18..., dimensions={0} | all-to-all | bytes 589824 | tf_op jit(solution)/shard_map/all_to_all | solution.py:353
  22.7 1.9 %all-gather.1 = f32[144,128]{1,0:T(8,128)S(1)} all-gather(f32[72,128]{1,0:T(8,128)S(1)} %shard_map.70), channel_id=3, replica_groups=mesh['tm'=32,'y'=4,'core'=2,'plane'=2] {'core'}, dimensions={0}, use_global_device_ids=true | all-gather | bytes 110592 | tf_op jit(solution)/shard_map/all_gather | solution.py:363
  24.6 0.0 copy-done.2
  24.6 1.3 shard_map.71
  25.8 0.0 copy-done
  25.8 1.0 shard_map.72
  26.8 12.2 %all_to_all.41.got_ref = f32[8,40,128]{2,1,0:T(8,128)S(1)} all-to-all(f32[8,40,128]{2,1,0:T(8,128)S(1)} %shard_map.72), channel_id=1, replica_groups={{0,256,16,272,32,288,48,304},{64,320,80,336,96,352,112,368},{160,416,17..., dimensions={0} | all-to-all | bytes 327680 | tf_op jit(solution)/shard_map/all_to_all | solution.py:353
  39.1 20.5 %all_to_all.42.got_ref = f32[4,40,128]{2,1,0:T(8,128)S(1)} all-to-all(f32[4,40,128]{2,1,0:T(8,128)S(1)} %shard_map.73), channel_id=1, replica_groups={{0,160,64,224},{256,416,320,480},{16,176,80,240},{272,432,336,496},{32,..., dimensions={0} | all-to-all | bytes 163840 | tf_op jit(solution)/shard_map/all_to_all | solution.py:353
  59.6 1.2 shard_map.74
  60.9 11.2 %all_to_all.43 = f32[8,32,128]{2,1,0:T(8,128)S(1)} all-to-all(f32[8,32,128]{2,1,0:T(8,128)S(1)} %get-tuple-element.9), channel_id=1, replica_groups={{0,256,16,272,32,288,48,304},{64,320,80,336,96,352,112,368},{160,416,17..., dimensions={0} | all-to-all | bytes 262144 | tf_op jit(solution)/shard_map/all_to_all | solution.py:353
  72.1 0.7 shard_map.75
  72.8 13.5 %all_to_all.44.got_ref = f32[8,136,128]{2,1,0:T(8,128)S(1)} all-to-all(f32[8,136,128]{2,1,0:T(8,128)S(1)} %shard_map.75), channel_id=1, replica_groups={{0,9,4,13,8,1,12,5},{2,11,6,15,10,3,14,7},{16,25,20,29,24,17,28,21},{18..., dimensions={0} | all-to-all | bytes 1114112 | tf_op jit(solution)/shard_map/all_to_all | solution.py:353
  86.3 1.9 %all-gather.2 = f32[272,128]{1,0:T(8,128)S(1)} all-gather(f32[136,128]{1,0:T(8,128)S(1)} %shard_map.76), channel_id=4, replica_groups=mesh['tm'=32,'y'=4,'core'=2,'plane'=2] {'core'}, dimensions={0}, use_global_device_ids=true | all-gather | bytes 208896 | tf_op jit(solution)/shard_map/all_gather | solution.py:363
  88.2 1.2 shard_map.77.rows_ref.all_c_ref
  89.4 1.0 shard_map.78
  90.4 10.5 %all_to_all.45.got_ref = f32[8,40,128]{2,1,0:T(8,128)S(1)} all-to-all(f32[8,40,128]{2,1,0:T(8,128)S(1)} %shard_map.78), channel_id=1, replica_groups={{0,256,16,272,32,288,48,304},{64,320,80,336,96,352,112,368},{160,416,17..., dimensions={0} | all-to-all | bytes 327680 | tf_op jit(solution)/shard_map/all_to_all | solution.py:353
  100.9 14.7 %all_to_all.46.got_ref = f32[4,40,128]{2,1,0:T(8,128)S(1)} all-to-all(f32[4,40,128]{2,1,0:T(8,128)S(1)} %shard_map.79), channel_id=1, replica_groups={{0,160,64,224},{256,416,320,480},{16,176,80,240},{272,432,336,496},{32,..., dimensions={0} | all-to-all | bytes 163840 | tf_op jit(solution)/shard_map/all_to_all | solution.py:353
  115.6 1.2 shard_map.80
  116.9 10.0 %all_to_all.47 = f32[8,32,128]{2,1,0:T(8,128)S(1)} all-to-all(f32[8,32,128]{2,1,0:T(8,128)S(1)} %shard_map.80), channel_id=1, replica_groups={{0,256,16,272,32,288,48,304},{64,320,80,336,96,352,112,368},{160,416,17..., dimensions={0} | all-to-all | bytes 262144 | tf_op jit(solution)/shard_map/all_to_all | solution.py:353
  126.9 1.2 shard_map.81
  (11 shorter events, 0.1 us)
Async XLA Ops:
  0.6 23.9 %copy-start.2 = (f32[128,256]{1,0:T(8,128)S(1)}, f32[128,256]{1,0:T(8,128)}, u32[]{:S(2)}) copy-start(f32[128,256]{1,0:T(8,128)} %traces_ref.3) | copy-start | bytes 393220
  0.6 0.7 copy-start.3
  1.3 23.2 %copy-start.4 = (s32[128]{0:T(128)S(1)}, s32[128]{0:T(128)}, u32[]{:S(2)}) copy-start(s32[128]{0:T(128)} %param.9) | copy-start | bytes 1540
  1.3 24.5 %copy-start = (bf16[8,512,256]{2,1,0:T(8,128)(2,1)S(1)}, bf16[8,512,256]{2,1,0:T(8,128)(2,1)}, u32[]{:S(2)}) copy-start(bf16[8,512,256]{2,1,0:T(8,128)(2,1)} %movie_ref.5) | copy-start | bytes 6291460
  5.9 53.7 %copy-start.1 = (f32[16,8,512]{2,1,0:T(8,128)S(1)}, f32[16,8,512]{2,1,0:T(8,128)}, u32[]{:S(2)}) copy-start(f32[16,8,512]{2,1,0:T(8,128)} %param.6) | copy-start | bytes 786436

commit v7 on v6

--- a/solution.py
+++ b/solution.py
@@ -222,12 +222,12 @@
     counts = spread(counts_ref)
     rows = rows_ref[...]
     gram = gram_chunk(counts, products(rows))
-    low = rows.T.astype(BF16)
-    patch, _ = patch_and_slot(counts, low.shape, 1)
+    low = rows.astype(BF16)
+    patch, _ = patch_and_slot(counts, low.shape, 0)
     zero = jnp.zeros_like(low)
     total = None
     for p in range(NP):
-        term = nn(movie_ref[p], jnp.where(patch == p, low, zero))
+        term = nt(movie_ref[p], jnp.where(patch == p, low, zero))
         total = term if p == 0 else total + term
     half = total.shape[0] // 2
     chunks = jnp.concatenate([total[:half], total[half:]], axis=1)

time: 129 us -> 129 us (level)
  no operation moved by 1% of the time
where the time goes in v7:
time: 129 us; the launch traced here: 128 us
  blocking collectives  115 us (89%)
  Pallas kernels  11.5 us (9%)
    all_to_all x8, blocking collectives, swap(): return lax.all_to_all(x, axes, 0, 0, tiled=True, axis_index_groups=members)  109 us
    pallas_call x14, Pallas kernels, call(): pl.pallas_call(kernel, out_shape=[jax.ShapeDtypeStruct(s, F32) for s in o...  11.5 us
    all_gather x3, blocking collectives, cores(): return lax.all_gather(x, 'core', axis=0, tiled=False)  5.68 us

profile of v7, /device:TPU:8, one launch (start us, length us, event | category | flops | bytes accessed | tf_op | source)
XLA Modules:
  0.0 128.1 jit_solution(9116726717572602372)
XLA Ops:
  0.7 0.7 copy-done.3
  1.3 2.6 %shard_map.68 = f32[2,72,128]{2,1,0:T(8,128)S(1)} custom-call(s32[1,8]{1,0:T(1,128)S(1)} %bitcast.16, f32[128,512]{1,0:T(8,128)} %bitcast.9, bf16[8,512,256]{2,1,0:T(8,128)(2,1)} %movie_ref.5), custom_call_target="tpu_custom_call" | custom-call | tf_op jit(solution)/shard_map/pallas_call | solution.py:332
  4.0 1.9 %all-gather = f32[4,72,128]{2,1,0:T(8,128)S(1)} all-gather(f32[2,72,128]{2,1,0:T(8,128)S(1)} %shard_map.68), channel_id=2, replica_groups=mesh['tm'=32,'y'=4,'core'=2,'plane'=2] {'core'}, dimensions={0}, use_global_device_ids=true | all-gather | bytes 221184 | tf_op jit(solution)/shard_map/all_gather | solution.py:363
  5.9 0.0 copy-start.1
  5.9 16.8 %all_to_all.40.got_ref = f32[8,72,128]{2,1,0:T(8,128)S(1)} all-to-all(f32[8,72,128]{2,1,0:T(8,128)S(1)} %shard_map.69), channel_id=1, replica_groups={{0,9,4,13,8,1,12,5},{2,11,6,15,10,3,14,7},{16,25,20,29,24,17,28,21},{18..., dimensions={0} | all-to-all | bytes 589824 | tf_op jit(solution)/shard_map/all_to_all | solution.py:353
  22.7 1.9 %all-gather.1 = f32[144,128]{1,0:T(8,128)S(1)} all-gather(f32[72,128]{1,0:T(8,128)S(1)} %shard_map.70), channel_id=3, replica_groups=mesh['tm'=32,'y'=4,'core'=2,'plane'=2] {'core'}, dimensions={0}, use_global_device_ids=true | all-gather | bytes 110592 | tf_op jit(solution)/shard_map/all_gather | solution.py:363
  24.6 1.3 shard_map.71
  25.8 0.0 copy-done
  25.8 1.0 shard_map.72
  26.8 12.2 %all_to_all.41.got_ref = f32[8,40,128]{2,1,0:T(8,128)S(1)} all-to-all(f32[8,40,128]{2,1,0:T(8,128)S(1)} %shard_map.72), channel_id=1, replica_groups={{0,256,16,272,32,288,48,304},{64,320,80,336,96,352,112,368},{160,416,17..., dimensions={0} | all-to-all | bytes 327680 | tf_op jit(solution)/shard_map/all_to_all | solution.py:353
  39.0 20.5 %all_to_all.42.got_ref = f32[4,40,128]{2,1,0:T(8,128)S(1)} all-to-all(f32[4,40,128]{2,1,0:T(8,128)S(1)} %shard_map.73), channel_id=1, replica_groups={{0,160,64,224},{256,416,320,480},{16,176,80,240},{272,432,336,496},{32,..., dimensions={0} | all-to-all | bytes 163840 | tf_op jit(solution)/shard_map/all_to_all | solution.py:353
  59.5 0.0 copy-done.1
  59.5 1.2 shard_map.74
  60.9 11.2 %all_to_all.43 = f32[8,32,128]{2,1,0:T(8,128)S(1)} all-to-all(f32[8,32,128]{2,1,0:T(8,128)S(1)} %get-tuple-element.9), channel_id=1, replica_groups={{0,256,16,272,32,288,48,304},{64,320,80,336,96,352,112,368},{160,416,17..., dimensions={0} | all-to-all | bytes 262144 | tf_op jit(solution)/shard_map/all_to_all | solution.py:353
  72.0 0.7 shard_map.75
  72.8 13.5 %all_to_all.44.got_ref = f32[8,136,128]{2,1,0:T(8,128)S(1)} all-to-all(f32[8,136,128]{2,1,0:T(8,128)S(1)} %shard_map.75), channel_id=1, replica_groups={{0,9,4,13,8,1,12,5},{2,11,6,15,10,3,14,7},{16,25,20,29,24,17,28,21},{18..., dimensions={0} | all-to-all | bytes 1114112 | tf_op jit(solution)/shard_map/all_to_all | solution.py:353
  86.3 1.9 %all-gather.2 = f32[272,128]{1,0:T(8,128)S(1)} all-gather(f32[136,128]{1,0:T(8,128)S(1)} %shard_map.76), channel_id=4, replica_groups=mesh['tm'=32,'y'=4,'core'=2,'plane'=2] {'core'}, dimensions={0}, use_global_device_ids=true | all-gather | bytes 208896 | tf_op jit(solution)/shard_map/all_gather | solution.py:363
  88.2 1.2 shard_map.77.rows_ref.all_c_ref
  89.4 1.0 shard_map.78
  90.4 10.5 %all_to_all.45.got_ref = f32[8,40,128]{2,1,0:T(8,128)S(1)} all-to-all(f32[8,40,128]{2,1,0:T(8,128)S(1)} %shard_map.78), channel_id=1, replica_groups={{0,256,16,272,32,288,48,304},{64,320,80,336,96,352,112,368},{160,416,17..., dimensions={0} | all-to-all | bytes 327680 | tf_op jit(solution)/shard_map/all_to_all | solution.py:353
  100.8 14.7 %all_to_all.46.got_ref = f32[4,40,128]{2,1,0:T(8,128)S(1)} all-to-all(f32[4,40,128]{2,1,0:T(8,128)S(1)} %shard_map.79), channel_id=1, replica_groups={{0,160,64,224},{256,416,320,480},{16,176,80,240},{272,432,336,496},{32,..., dimensions={0} | all-to-all | bytes 163840 | tf_op jit(solution)/shard_map/all_to_all | solution.py:353
  115.6 1.2 shard_map.80
  116.8 10.0 %all_to_all.47 = f32[8,32,128]{2,1,0:T(8,128)S(1)} all-to-all(f32[8,32,128]{2,1,0:T(8,128)S(1)} %shard_map.80), channel_id=1, replica_groups={{0,256,16,272,32,288,48,304},{64,320,80,336,96,352,112,368},{160,416,17..., dimensions={0} | all-to-all | bytes 262144 | tf_op jit(solution)/shard_map/all_to_all | solution.py:353
  126.8 1.2 shard_map.81
  (11 shorter events, 0.1 us)
Async XLA Ops:
  0.6 23.9 %copy-start.2 = (f32[128,256]{1,0:T(8,128)S(1)}, f32[128,256]{1,0:T(8,128)}, u32[]{:S(2)}) copy-start(f32[128,256]{1,0:T(8,128)} %traces_ref.3) | copy-start | bytes 393220
  0.6 0.7 copy-start.3
  1.3 23.2 %copy-start.4 = (s32[128]{0:T(128)S(1)}, s32[128]{0:T(128)}, u32[]{:S(2)}) copy-start(s32[128]{0:T(128)} %param.9) | copy-start | bytes 1540
  1.3 24.5 %copy-start = (bf16[8,512,256]{2,1,0:T(8,128)(2,1)S(1)}, bf16[8,512,256]{2,1,0:T(8,128)(2,1)}, u32[]{:S(2)}) copy-start(bf16[8,512,256]{2,1,0:T(8,128)(2,1)} %movie_ref.5) | copy-start | bytes 6291460
  5.9 53.6 %copy-start.1 = (f32[16,8,512]{2,1,0:T(8,128)S(1)}, f32[16,8,512]{2,1,0:T(8,128)}, u32[]{:S(2)}) copy-start(f32[16,8,512]{2,1,0:T(8,128)} %param.6) | copy-start | bytes 786436
